TPU v7x, 32 devices: a whole 2x2x4 slice. The times are simulated.
32 devices in a mesh: grp: 4 (over x, core), dev: 8 (over z, y).
Axes of the slice: x: 2, y: 2, z: 4, core: 2. Of those that a mesh axis runs over, the one named last changes fastest.
Arguments:
- right_side: float32 [3072, 512], P(('grp', 'dev')), may hold values from -6 to 6
- ghost_rows: int32 [64, 24], P(('grp', 'dev')), may hold values from 0 to 95
- cols_one: int32 [3072, 2], P(('grp', 'dev')), may hold values from 0 to 143
- diag_one: float32 [3072, 4096], P(('grp', 'dev')), may hold values from -1 to 7
- offd_one: float32 [3072, 2, 4096], P(('grp', 'dev')), may hold values from -0.75 to 0.75
- prol_one: float32 [3072, 4096], P(('grp', 'dev')), may hold values from -0.75 to 0.75
- agg_one: int32 [3072], P(('grp', 'dev')), may hold values from 0 to 95
- cols_two: int32 [1536, 2], P(('grp', 'dev')), may hold values from 0 to 287, as said below
- diag_two: float32 [1536, 4096], P(('grp', 'dev')), may hold values from -1 to 7
- offd_two: float32 [1536, 2, 4096], P(('grp', 'dev')), may hold values from -0.75 to 0.75
- prol_two: float32 [1536, 4096], P(('grp', 'dev')), may hold values from -0.375 to 0.375
- agg_two: int32 [1536], P(('grp', 'dev')), may hold values from 0 to 31
- cols_three: int32 [32, 2], replicated, may hold values from 0 to 31
- diag_three: float32 [32, 4096], replicated, may hold values from -1 to 7
- offd_three: float32 [32, 2, 4096], replicated, may hold values from -0.75 to 0.75
Outputs:
- solution: float32 [3072, 512], P(('grp', 'dev'))
- coarse_solution: float32 [32, 512], replicated
Inputs may be any that keep to these rules, and one draw needn't show every extreme that they name: `cols_two`: columns k = 0, 2, 4, ... read only pair blocks p - 1 and p (values below 192); columns k = 1, 3, 5, ... read only pair blocks p and p + 1 (values from 96 on).
All inputs are finite; a program needn't handle non-finite values.
Results may differ from a plain program's by a relative error of at most 0.00011.
Values sent between devices are 32-bit elements; how exact they have to be, the bound alone decides.
A program may use at most 128 MiB of HBM per device.

v0:
```python
import jax
import jax.numpy as jnp
from jax import lax
from jax.sharding import PartitionSpec as P

TILE = 64
LOADS = 8
ROWS = 96
COARSE = 32
DEGREE = 3
COARSE_DEGREE = 8
HALF = 48


cheb_low = 1.0
cheb_high = 9.0
highest = lax.Precision.HIGHEST


def partner(value, axis, bit):
    mask = 2**bit
    pairs = [(source, source ^ mask) for source in range(lax.axis_size(axis))]
    return lax.ppermute(value, axis, pairs)


def shifted(value, axis, steps):
    count = lax.axis_size(axis)
    initial, last = (max(0, -steps), min(count, count - steps))
    return lax.ppermute(value, axis, [(source, source + steps) for source in range(initial, last)])


def padded_2(cells, sides, width):
    for axis, dim in sides:
        count = lax.axis_size(axis)
        ends = count - 1
        head = lax.slice_in_dim(cells, 0, width, axis=dim)
        tail = lax.slice_in_dim(cells, cells.shape[dim] - width, cells.shape[dim], axis=dim)
        cells = jnp.concatenate(
            [
                lax.ppermute(tail, axis, [(i, (i + 1) % count) for i in range(ends)]),
                cells,
                lax.ppermute(head, axis, [((i + 1) % count, i) for i in range(ends)]),
            ],
            axis=dim,
        )
    return cells


def as_tiles(flat_tile):
    return flat_tile.reshape(flat_tile.shape[:-1] + (TILE, TILE))


def apply_tiles(diag_part, offd_part, own_rows, picked):
    own_rows = own_rows.reshape(own_rows.shape[0], LOADS, TILE)
    picked = picked.reshape(picked.shape[0], picked.shape[1], LOADS, TILE)
    result = jnp.einsum("iab,ivb->iva", as_tiles(diag_part), own_rows, precision=highest)
    result = result + jnp.einsum("ikab,ikvb->iva", as_tiles(offd_part), picked, precision=highest)
    return result.reshape(result.shape[0], LOADS * TILE)


def prolong(prol, coarse_rows):
    coarse_rows = coarse_rows.reshape(coarse_rows.shape[0], LOADS, TILE)
    result = jnp.einsum("iab,ivb->iva", as_tiles(prol), coarse_rows, precision=highest)
    return result.reshape(result.shape[0], LOADS * TILE)


def restrict(prol, aggregate, fine_rows, row_count):
    fine_rows = fine_rows.reshape(fine_rows.shape[0], LOADS, TILE)
    terms = jnp.einsum("iab,iva->ivb", as_tiles(prol), fine_rows, precision=highest)
    terms = terms.reshape(terms.shape[0], LOADS * TILE)
    one_hot = (aggregate[None, :] == jnp.arange(row_count, dtype=jnp.int32)[:, None]).astype(
        jnp.float32
    )
    return jnp.dot(one_hot, terms, precision=highest)


def chebyshev(operate, solution, residual, degree, finish):
    center = 0.5 * (cheb_high + cheb_low)
    radius = 0.5 * (cheb_high - cheb_low)
    sigma_value = center / radius
    rho_now = 1.0 / sigma_value
    direction = residual / center
    solution = solution + direction
    for turn_index in range(degree - 1):
        residual = residual - operate(direction)
        rho_next = 1.0 / (2.0 * sigma_value - rho_now)
        direction = rho_next * rho_now * direction + 2.0 * rho_next / radius * residual
        solution = solution + direction
        rho_now = rho_next
    if finish:
        residual = residual - operate(direction)
    return (solution, residual)


def ordered_pair(mine, other, lower_half):
    return jnp.where(
        lower_half, jnp.concatenate([mine, other], 0), jnp.concatenate([other, mine], 0)
    )


def assemble(own_part, lower_half):
    other = partner(own_part, "dev", 0)
    return ordered_pair(own_part, other, lower_half)


def pair_reader(cols, vector):
    left_pair = shifted(vector, ("grp", "dev"), 2)
    right_pair = shifted(vector, ("grp", "dev"), -2)
    return jnp.concatenate([left_pair, vector, right_pair], 0)[cols]


def body(
    right_side,
    ghost_rows,
    cols_one,
    diag_one,
    offd_one,
    prol_one,
    agg_one,
    cols_two,
    diag_two,
    offd_two,
    prol_two,
    agg_two,
    cols_three,
    diag_three,
    offd_three,
):
    half_index = lax.axis_index("dev") % 2
    lower_half = half_index == 0

    def windowed(vector):
        padded = padded_2(vector, ((("grp", "dev"), 0),), ROWS)
        return jnp.concatenate(
            [padded[:ROWS][ghost_rows[0]], vector, padded[2 * ROWS :][ghost_rows[1]]], 0
        )

    def level_one(vector):
        window = windowed(vector)
        return apply_tiles(diag_one, offd_one, vector, window[cols_one])

    def level_two(vector):
        own_rows = lax.dynamic_slice_in_dim(vector, half_index * HALF, HALF, 0)
        return assemble(
            apply_tiles(diag_two, offd_two, own_rows, pair_reader(cols_two, vector)), lower_half
        )

    def level_three(vector):
        return apply_tiles(diag_three, offd_three, vector, vector[cols_three])

    smooth_one, res_one = chebyshev(level_one, jnp.zeros_like(right_side), right_side, DEGREE, True)
    part_sum = restrict(prol_one, agg_one, res_one, ROWS)
    rhs_two = part_sum + partner(part_sum, "dev", 0)
    smooth_two, res_two = chebyshev(level_two, jnp.zeros_like(rhs_two), rhs_two, DEGREE, True)
    own_residual = lax.dynamic_slice_in_dim(res_two, half_index * HALF, HALF, 0)
    coarse_rhs = lax.psum(restrict(prol_two, agg_two, own_residual, COARSE), ("grp", "dev"))
    coarse_solution = chebyshev(
        level_three, jnp.zeros_like(coarse_rhs), coarse_rhs, COARSE_DEGREE, False
    )[0]
    corrected_two = smooth_two + assemble(prolong(prol_two, coarse_solution[agg_two]), lower_half)
    smoothed_two = chebyshev(
        level_two, corrected_two, rhs_two - level_two(corrected_two), DEGREE, False
    )[0]
    corrected_one = smooth_one + prolong(prol_one, smoothed_two[agg_one])
    solution = chebyshev(
        level_one, corrected_one, right_side - level_one(corrected_one), DEGREE, False
    )[0]
    return (solution, coarse_solution)


def solution(mesh):
    return jax.shard_map(
        body,
        mesh=mesh,
        in_specs=(
            P(("grp", "dev"), None),
            P(("grp", "dev"), None),
            P(("grp", "dev"), None),
            P(("grp", "dev"), None),
            P(("grp", "dev"), None, None),
            P(("grp", "dev"), None),
            P(("grp", "dev")),
            P(("grp", "dev"), None),
            P(("grp", "dev"), None),
            P(("grp", "dev"), None, None),
            P(("grp", "dev"), None),
            P(("grp", "dev")),
            P(),
            P(),
            P(),
        ),
        out_specs=(P(("grp", "dev"), None), P()),
        check_vma=False,
    )
```

profile of v0, /device:TPU:29, one launch (start us, length us, event | category | flops | bytes accessed | tf_op | source)
XLA Modules:
  0.0 739.6 jit_solution(13305348373156061359)
XLA Ops:
  10.3 7.0 collective-permute-start
  21.2 4.0 copy.22
  25.6 6.3 copy.24
  31.9 7.7 %copy.25 = f32[96,2,64,64]{3,2,1,0:T(8,128)} copy(f32[96,2,64,64]{0,3,2,1:T(8,128)} %bitcast.196) | data formatting | bytes 6291456 | tf_op jit(solution)/shard_map/reshape | solution.py:50
  42.4 5.0 copy.43
  47.4 6.7 fusion.33
  62.5 8.8 %fusion = f32[96,8,64]{2,1,0:T(8,128)} fusion(f32[96,8,64]{2,1,0:T(8,128)} %fusion.33, f32[96,2,8,64]{3,2,1,0:T(8,128)} %reshape.317, f32[96,2,64,64]{3,2,1,0:T(8,128)} %copy.25), kind=kOutput, calls=%fused_computation.39 | convolution fusion | flops 75546624 | bytes 3932160 | tf_op jit(solution)/shard_map/ikab,ikvb->iva/dot_general | solution.py:57
  77.8 7.5 %collective-permute-start.2 = (f32[96,512]{1,0:T(8,128)S(1)}, f32[96,512]{1,0:T(8,128)}, u32[]{:S(2)}, u32[]{:S(2)}) collective-permute-start(f32[96,512]{1,0:T(8,128)S(1)} %get-tuple-element.24), channel_id=1, source_target_pairs={{0,1},{1,2},{2,3},{3,4},{4,5},{5,6},{6,7},{7,8},{8,9},{9,10},{10,1... | collective-permute-start | bytes 589832 | tf_op jit(solution)/shard_map/ppermute | solution.py:40
  87.1 6.7 fusion.34
  102.2 8.9 %fusion.1 = f32[96,8,64]{2,1,0:T(8,128)} fusion(f32[96,8,64]{2,1,0:T(8,128)} %fusion.34, f32[96,2,8,64]{3,2,1,0:T(8,128)} %reshape.321, f32[96,2,64,64]{3,2,1,0:T(8,128)} %copy.25), kind=kOutput, calls=%fused_computation.40 | convolution fusion | flops 75546624 | bytes 3932160 | tf_op jit(solution)/shard_map/ikab,ikvb->iva/dot_general | solution.py:57
  120.3 7.6 %collective-permute-start.4 = (f32[96,512]{1,0:T(8,128)}, f32[96,512]{1,0:T(8,128)}, u32[]{:S(2)}, u32[]{:S(2)}) collective-permute-start(f32[96,512]{1,0:T(8,128)} %get-tuple-element.22), channel_id=1, source_target_pairs={{0,1},{1,2},{2,3},{3,4},{4,5},{5,6},{6,7},{7,8},{8,9},{9,10},{10,1... | collective-permute-start | bytes 589832 | tf_op jit(solution)/shard_map/ppermute | solution.py:40
  129.8 6.7 fusion.35
  141.6 9.0 %fusion.2 = f32[96,8,64]{2,1,0:T(8,128)} fusion(f32[96,8,64]{2,1,0:T(8,128)} %fusion.35, f32[96,2,8,64]{3,2,1,0:T(8,128)} %reshape.324, f32[96,2,64,64]{3,2,1,0:T(8,128)} %copy.25), kind=kOutput, calls=%fused_computation.41 | convolution fusion | flops 75546624 | bytes 3932160 | tf_op jit(solution)/shard_map/ikab,ikvb->iva/dot_general | solution.py:57
  157.9 4.5 fusion.36
  164.3 3.0 reshape.332
  173.9 6.3 collective-permute-start.7
  190.0 3.7 convolution_bitcast_fusion.11
  193.7 4.2 convolution_add_fusion.5
  200.6 3.3 collective-permute-done.9
  207.5 6.4 collective-permute-start.10
  224.8 3.7 convolution_bitcast_fusion.10
  228.5 3.2 convolution_add_fusion.4
  241.7 7.7 %collective-permute-start.13 = (f32[96,512]{1,0:T(8,128)}, f32[96,512]{1,0:T(8,128)}, u32[]{:S(2)}, u32[]{:S(2)}) collective-permute-start(f32[96,512]{1,0:T(8,128)} %get-tuple-element.18), channel_id=1, source_target_pairs={{0,2},{1,3},{2,4},{3,5},{4,6},{5,7},{6,8},{7,9},{8,10},{9,11},{10,... | collective-permute-start | bytes 589832 | tf_op jit(solution)/shard_map/ppermute | solution.py:29
  258.9 3.7 convolution_bitcast_fusion.9
  262.6 4.2 convolution_add_fusion.3
  273.7 3.5 fusion.37
  282.0 3.6 reshape.346
  285.6 113.4 %all-reduce.2.cloned.1.call-done = f32[32,512]{1,0:T(8,128)} async-done(((f32[32,512]{1,0:T(8,128)}), f32[32,512]{1,0:T(8,128)}) %all-reduce.2.cloned.1.call-update) | async-done | bytes 65552 | tf_op jit(solution)/shard_map/psum | solution.py:156
  403.0 3.0 fusion.38
  406.0 4.0 fusion.6
  413.0 3.6 fusion.39
  417.6 4.0 fusion.7
  425.5 3.0 fusion.40
  430.3 4.1 fusion.8
  442.2 4.1 fusion.9
  450.1 3.7 fusion.42
  455.5 4.0 fusion.10
  464.7 3.7 fusion.43
  470.0 4.0 fusion.11
  479.2 3.7 fusion.44
  484.6 4.0 fusion.12
  492.9 4.8 fusion.45
  499.0 3.7 collective-permute-done.16
  506.4 6.6 collective-permute-start.17
  523.7 3.7 convolution_bitcast_fusion.8
  527.4 3.3 convolution_add_fusion.2
  532.0 3.2 collective-permute-done.19
  538.5 8.1 %collective-permute-start.20 = (f32[96,512]{1,0:T(8,128)}, f32[96,512]{1,0:T(8,128)}, u32[]{:S(2)}, u32[]{:S(2)}) collective-permute-start(f32[96,512]{1,0:T(8,128)} %broadcast_multiply_fusion.1), channel_id=1, source_target_pairs={{0,2},{1,3},{2,4},{3,5},{4,6},{5,7},{6,8},{7,9},{8,10},{9,11},{10,... | collective-permute-start | bytes 589832 | tf_op jit(solution)/shard_map/ppermute | solution.py:29
  557.2 3.7 convolution_bitcast_fusion.7
  560.9 3.3 convolution_add_fusion.1
  566.1 4.6 collective-permute-done.22
  575.0 7.5 %collective-permute-start.23 = (f32[96,512]{1,0:T(8,128)}, f32[96,512]{1,0:T(8,128)}, u32[]{:S(2)}, u32[]{:S(2)}) collective-permute-start(f32[96,512]{1,0:T(8,128)} %multiply_add_fusion.1), channel_id=1, source_target_pairs={{0,2},{1,3},{2,4},{3,5},{4,6},{5,7},{6,8},{7,9},{8,10},{9,11},{10,... | collective-permute-start | bytes 589832 | tf_op jit(solution)/shard_map/ppermute | solution.py:29
  592.5 3.7 convolution_bitcast_fusion.6
  599.3 3.7 collective-permute-done.25
  606.1 7.9 %fusion.46 = f32[96,8,64]{2,1,0:T(8,128)} fusion(f32[96,8,64]{2,1,0:T(8,128)} %copy.48, f32[96,64,64]{2,1,0:T(8,128)} %copy.43), kind=kOutput, calls=%fused_computation.167 | convolution fusion | flops 37748736 | bytes 1966080 | tf_op jit(solution)/shard_map/iab,ivb->iva/dot_general | solution.py:63
  622.7 8.6 %collective-permute-start.26 = (f32[96,512]{1,0:T(8,128)}, f32[96,512]{1,0:T(8,128)}, u32[]{:S(2)}, u32[]{:S(2)}) collective-permute-start(f32[96,512]{1,0:T(8,128)} %add_add_fusion.1), channel_id=1, source_target_pairs={{0,1},{1,2},{2,3},{3,4},{4,5},{5,6},{6,7},{7,8},{8,9},{9,10},{10,1... | collective-permute-start | bytes 589832 | tf_op jit(solution)/shard_map/ppermute | solution.py:40
  632.2 6.8 fusion.47
  647.5 8.9 %fusion.3 = f32[96,8,64]{2,1,0:T(8,128)} fusion(f32[96,8,64]{2,1,0:T(8,128)} %fusion.47, f32[96,2,8,64]{3,2,1,0:T(8,128)} %reshape.380, f32[96,2,64,64]{3,2,1,0:T(8,128)} %copy.25), kind=kOutput, calls=%fused_computation.42 | convolution fusion | flops 75546624 | bytes 3932160 | tf_op jit(solution)/shard_map/ikab,ikvb->iva/dot_general | solution.py:57
  664.7 7.5 %collective-permute-start.28 = (f32[96,512]{1,0:T(8,128)}, f32[96,512]{1,0:T(8,128)}, u32[]{:S(2)}, u32[]{:S(2)}) collective-permute-start(f32[96,512]{1,0:T(8,128)} %get-tuple-element.4), channel_id=1, source_target_pairs={{0,1},{1,2},{2,3},{3,4},{4,5},{5,6},{6,7},{7,8},{8,9},{9,10},{10,1... | collective-permute-start | bytes 589832 | tf_op jit(solution)/shard_map/ppermute | solution.py:40
  673.1 6.8 fusion.48
  688.4 8.9 %fusion.4 = f32[96,8,64]{2,1,0:T(8,128)} fusion(f32[96,8,64]{2,1,0:T(8,128)} %fusion.48, f32[96,2,8,64]{3,2,1,0:T(8,128)} %reshape.383, f32[96,2,64,64]{3,2,1,0:T(8,128)} %copy.25), kind=kOutput, calls=%fused_computation.43 | convolution fusion | flops 75546624 | bytes 3932160 | tf_op jit(solution)/shard_map/ikab,ikvb->iva/dot_general | solution.py:57
  703.7 7.5 %collective-permute-start.30 = (f32[96,512]{1,0:T(8,128)S(1)}, f32[96,512]{1,0:T(8,128)}, u32[]{:S(2)}, u32[]{:S(2)}) collective-permute-start(f32[96,512]{1,0:T(8,128)S(1)} %get-tuple-element.2), channel_id=1, source_target_pairs={{0,1},{1,2},{2,3},{3,4},{4,5},{5,6},{6,7},{7,8},{8,9},{9,10},{10,1... | collective-permute-start | bytes 589832 | tf_op jit(solution)/shard_map/ppermute | solution.py:40
  713.1 6.7 fusion.49
  724.2 7.1 fusion.5
  (313 shorter events, 272.6 us)
Async XLA Ops:
  7.2 391.9 %all-reduce.2.cloned.1.call-start = ((), (), s32[]{:S(2)}) async-start(), calls=%async_computation | async-start | bytes 131072 | tf_op jit(solution)/shard_map/psum | solution.py:156
  8.2 17.1 %copy-start.17 = (f32[96,512]{1,0:T(8,128)}, f32[96,512]{1,0:T(8,128)S(1)}, u32[]{:S(2)}) copy-start(f32[96,512]{1,0:T(8,128)S(1)} %broadcast_multiply_fusion.3) | copy-start | bytes 589828
  8.2 46.0 %collective-permute-start.1 = (f32[96,512]{1,0:T(8,128)S(1)}, f32[96,512]{1,0:T(8,128)}, u32[]{:S(2)}, u32[]{:S(2)}) collective-permute-start(f32[96,512]{1,0:T(8,128)S(1)} %broadcast_multiply_fusion.3), channel_id=1, source_target_pairs={{1,0},{2,1},{3,2},{4,3},{5,4},{6,5},{7,6},{8,7},{9,8},{10,9},{11,1... | collective-permute-start | bytes 589832 | tf_op jit(solution)/shard_map/ppermute | solution.py:42
  10.3 45.4 %collective-permute-start = (f32[96,512]{1,0:T(8,128)S(1)}, f32[96,512]{1,0:T(8,128)}, u32[]{:S(2)}, u32[]{:S(2)}) collective-permute-start(f32[96,512]{1,0:T(8,128)S(1)} %broadcast_multiply_fusion.3), channel_id=1, source_target_pairs={{0,1},{1,2},{2,3},{3,4},{4,5},{5,6},{6,7},{7,8},{8,9},{9,10},{10,1... | collective-permute-start | bytes 589832 | tf_op jit(solution)/shard_map/ppermute | solution.py:40
  21.2 4.1 copy-start.34
  21.2 4.1 copy-start.35
  25.3 104.5 %copy-start = (f32[96,64,64]{2,1,0:T(8,128)}, f32[96,64,64]{2,1,0:T(8,128)S(1)}, u32[]{:S(2)}) copy-start(f32[96,64,64]{2,1,0:T(8,128)S(1)} %copy.22) | copy-start | bytes 4718596
  54.1 82.4 %copy-start.33 = (s32[1024]{0:T(1024)}, s32[1024]{0:T(1024)S(1)}, u32[]{:S(2)}) copy-start(s32[1024]{0:T(1024)S(1)} %get-tuple-element.28) | copy-start | bytes 12292
  75.1 20.4 %copy-start.12 = (f32[96,512]{1,0:T(8,128)}, f32[96,512]{1,0:T(8,128)S(1)}, u32[]{:S(2)}) copy-start(f32[96,512]{1,0:T(8,128)S(1)} %get-tuple-element.24) | copy-start | bytes 589828
  75.9 18.0 %collective-permute-start.3 = (f32[96,512]{1,0:T(8,128)S(1)}, f32[96,512]{1,0:T(8,128)}, u32[]{:S(2)}, u32[]{:S(2)}) collective-permute-start(f32[96,512]{1,0:T(8,128)S(1)} %get-tuple-element.24), channel_id=1, source_target_pairs={{1,0},{2,1},{3,2},{4,3},{5,4},{6,5},{7,6},{8,7},{9,8},{10,9},{11,1... | collective-permute-start | bytes 589832 | tf_op jit(solution)/shard_map/ppermute | solution.py:42
  77.8 17.6 %collective-permute-start.2 = (f32[96,512]{1,0:T(8,128)S(1)}, f32[96,512]{1,0:T(8,128)}, u32[]{:S(2)}, u32[]{:S(2)}) collective-permute-start(f32[96,512]{1,0:T(8,128)S(1)} %get-tuple-element.24), channel_id=1, source_target_pairs={{0,1},{1,2},{2,3},{3,4},{4,5},{5,6},{6,7},{7,8},{8,9},{9,10},{10,1... | collective-permute-start | bytes 589832 | tf_op jit(solution)/shard_map/ppermute | solution.py:40
  102.2 12.5 %copy-start.13 = (f32[96,512]{1,0:T(8,128)S(1)}, f32[96,512]{1,0:T(8,128)}, u32[]{:S(2)}) copy-start(f32[96,512]{1,0:T(8,128)} %copy-done.12) | copy-start | bytes 589828
  116.5 23.1 %copy-start.18 = (f32[96,512]{1,0:T(8,128)S(1)}, f32[96,512]{1,0:T(8,128)}, u32[]{:S(2)}) copy-start(f32[96,512]{1,0:T(8,128)} %get-tuple-element.22) | copy-start | bytes 589828
  118.3 18.2 %collective-permute-start.5 = (f32[96,512]{1,0:T(8,128)}, f32[96,512]{1,0:T(8,128)}, u32[]{:S(2)}, u32[]{:S(2)}) collective-permute-start(f32[96,512]{1,0:T(8,128)} %get-tuple-element.22), channel_id=1, source_target_pairs={{1,0},{2,1},{3,2},{4,3},{5,4},{6,5},{7,6},{8,7},{9,8},{10,9},{11,1... | collective-permute-start | bytes 589832 | tf_op jit(solution)/shard_map/ppermute | solution.py:42
  120.3 17.8 %collective-permute-start.4 = (f32[96,512]{1,0:T(8,128)}, f32[96,512]{1,0:T(8,128)}, u32[]{:S(2)}, u32[]{:S(2)}) collective-permute-start(f32[96,512]{1,0:T(8,128)} %get-tuple-element.22), channel_id=1, source_target_pairs={{0,1},{1,2},{2,3},{3,4},{4,5},{5,6},{6,7},{7,8},{8,9},{9,10},{10,1... | collective-permute-start | bytes 589832 | tf_op jit(solution)/shard_map/ppermute | solution.py:40
  141.6 12.6 %copy-start.20 = (f32[96,512]{1,0:T(8,128)S(1)}, f32[96,512]{1,0:T(8,128)}, u32[]{:S(2)}) copy-start(f32[96,512]{1,0:T(8,128)} %get-tuple-element.23) | copy-start | bytes 589828
  141.6 16.3 %copy-start.8 = (f32[96,64,64]{2,1,0:T(8,128)S(1)}, f32[96,64,64]{2,1,0:T(8,128)}, u32[]{:S(2)}) copy-start(f32[96,64,64]{2,1,0:T(8,128)} %copy.43) | copy-start | bytes 4718596
  154.2 9.3 %copy-start.39 = (s32[96]{0:T(128)S(1)}, s32[96]{0:T(128)}, u32[]{:S(2)}) copy-start(s32[96]{0:T(128)} %param.21) | copy-start | bytes 1156
  155.9 8.2 %copy-start.36 = (s32[48,2]{0,1:T(2,128)S(1)}, s32[48,2]{0,1:T(2,128)}, u32[]{:S(2)}) copy-start(s32[48,2]{0,1:T(2,128)} %param.22) | copy-start | bytes 1156
  164.0 6.3 copy-start.28
  164.0 6.3 collective-permute-start.6
  172.0 65.8 %copy-start.10 = (f32[96,512]{1,0:T(8,128)}, f32[96,512]{1,0:T(8,128)S(1)}, u32[]{:S(2)}) copy-start(f32[96,512]{1,0:T(8,128)S(1)} %get-tuple-element.21) | copy-start | bytes 589828
  172.0 11.7 %collective-permute-start.8 = (f32[96,512]{1,0:T(8,128)}, f32[96,512]{1,0:T(8,128)}, u32[]{:S(2)}, u32[]{:S(2)}) collective-permute-start(f32[96,512]{1,0:T(8,128)} %get-tuple-element.20), channel_id=1, source_target_pairs={{2,0},{3,1},{4,2},{5,3},{6,4},{7,5},{8,6},{9,7},{10,8},{11,9},{12,... | collective-permute-start | bytes 589832 | tf_op jit(solution)/shard_map/ppermute | solution.py:29
  173.9 9.8 %collective-permute-start.7 = (f32[96,512]{1,0:T(8,128)}, f32[96,512]{1,0:T(8,128)}, u32[]{:S(2)}, u32[]{:S(2)}) collective-permute-start(f32[96,512]{1,0:T(8,128)} %get-tuple-element.20), channel_id=1, source_target_pairs={{0,2},{1,3},{2,4},{3,5},{4,6},{5,7},{6,8},{7,9},{8,10},{9,11},{10,... | collective-permute-start | bytes 589832 | tf_op jit(solution)/shard_map/ppermute | solution.py:29
  198.9 5.0 collective-permute-start.9
  205.6 12.2 %collective-permute-start.11 = (f32[96,512]{1,0:T(8,128)}, f32[96,512]{1,0:T(8,128)}, u32[]{:S(2)}, u32[]{:S(2)}) collective-permute-start(f32[96,512]{1,0:T(8,128)} %multiply_add_fusion.3), channel_id=1, source_target_pairs={{2,0},{3,1},{4,2},{5,3},{6,4},{7,5},{8,6},{9,7},{10,8},{11,9},{12,... | collective-permute-start | bytes 589832 | tf_op jit(solution)/shard_map/ppermute | solution.py:29
  207.5 11.0 %collective-permute-start.10 = (f32[96,512]{1,0:T(8,128)}, f32[96,512]{1,0:T(8,128)}, u32[]{:S(2)}, u32[]{:S(2)}) collective-permute-start(f32[96,512]{1,0:T(8,128)} %multiply_add_fusion.3), channel_id=1, source_target_pairs={{0,2},{1,3},{2,4},{3,5},{4,6},{5,7},{6,8},{7,9},{8,10},{9,11},{10,... | collective-permute-start | bytes 589832 | tf_op jit(solution)/shard_map/ppermute | solution.py:29
  224.8 3.7 copy-start.3
  224.8 3.7 copy-start.26
  224.8 10.3 %copy-start.37 = (s32[32,2]{0,1:T(2,128)S(1)}, s32[32,2]{0,1:T(2,128)}, u32[]{:S(2)}) copy-start(s32[32,2]{0,1:T(2,128)} %param.27) | copy-start | bytes 772
  224.8 24.7 %copy-start.38 = (s32[48]{0:T(128)S(1)}, s32[48]{0:T(128)}, u32[]{:S(2)}) copy-start(s32[48]{0:T(128)} %param.26) | copy-start | bytes 580
  233.4 4.4 collective-permute-start.12
  239.8 14.5 %collective-permute-start.14 = (f32[96,512]{1,0:T(8,128)}, f32[96,512]{1,0:T(8,128)S(1)}, u32[]{:S(2)}, u32[]{:S(2)}) collective-permute-start(f32[96,512]{1,0:T(8,128)} %get-tuple-element.18), channel_id=1, source_target_pairs={{2,0},{3,1},{4,2},{5,3},{6,4},{7,5},{8,6},{9,7},{10,8},{11,9},{12,... | collective-permute-start | bytes 589832 | tf_op jit(solution)/shard_map/ppermute | solution.py:29
  241.7 12.5 %collective-permute-start.13 = (f32[96,512]{1,0:T(8,128)}, f32[96,512]{1,0:T(8,128)}, u32[]{:S(2)}, u32[]{:S(2)}) collective-permute-start(f32[96,512]{1,0:T(8,128)} %get-tuple-element.18), channel_id=1, source_target_pairs={{0,2},{1,3},{2,4},{3,5},{4,6},{5,7},{6,8},{7,9},{8,10},{9,11},{10,... | collective-permute-start | bytes 589832 | tf_op jit(solution)/shard_map/ppermute | solution.py:29
  258.9 13.1 %copy-start.22 = (f32[96,512]{1,0:T(8,128)S(1)}, f32[96,512]{1,0:T(8,128)}, u32[]{:S(2)}) copy-start(f32[96,512]{1,0:T(8,128)} %get-tuple-element.19) | copy-start | bytes 589828
  267.8 4.2 collective-permute-start.15
  399.0 12.0 %copy-start.30 = (f32[32,512]{1,0:T(8,128)S(1)}, f32[32,512]{1,0:T(8,128)}, u32[]{:S(2)}) copy-start(f32[32,512]{1,0:T(8,128)} %all-reduce.2.cloned.1.call-done) | copy-start | bytes 196612
  447.9 13.2 %copy-start.32 = (f32[32,512]{1,0:T(8,128)S(1)}, f32[32,512]{1,0:T(8,128)}, u32[]{:S(2)}) copy-start(f32[32,512]{1,0:T(8,128)} %get-tuple-element.11) | copy-start | bytes 196612
  491.2 30.7 %copy-start.9 = (f32[32,512]{1,0:T(8,128)}, f32[32,512]{1,0:T(8,128)S(1)}, u32[]{:S(2)}) copy-start(f32[32,512]{1,0:T(8,128)S(1)} %add_add_fusion.2) | copy-start | bytes 196612
  491.2 11.5 %copy-start.11 = (f32[96,512]{1,0:T(8,128)S(1)}, f32[96,512]{1,0:T(8,128)}, u32[]{:S(2)}) copy-start(f32[96,512]{1,0:T(8,128)} %copy-done.10) | copy-start | bytes 589828
  498.6 4.0 collective-permute-start.16
  504.5 12.2 %collective-permute-start.18 = (f32[96,512]{1,0:T(8,128)}, f32[96,512]{1,0:T(8,128)}, u32[]{:S(2)}, u32[]{:S(2)}) collective-permute-start(f32[96,512]{1,0:T(8,128)} %fusion.15), channel_id=1, source_target_pairs={{2,0},{3,1},{4,2},{5,3},{6,4},{7,5},{8,6},{9,7},{10,8},{11,9},{12,... | collective-permute-start | bytes 589832 | tf_op jit(solution)/shard_map/ppermute | solution.py:29
  506.4 11.0 %collective-permute-start.17 = (f32[96,512]{1,0:T(8,128)}, f32[96,512]{1,0:T(8,128)}, u32[]{:S(2)}, u32[]{:S(2)}) collective-permute-start(f32[96,512]{1,0:T(8,128)} %fusion.15), channel_id=1, source_target_pairs={{0,2},{1,3},{2,4},{3,5},{4,6},{5,7},{6,8},{7,9},{8,10},{9,11},{10,... | collective-permute-start | bytes 589832 | tf_op jit(solution)/shard_map/ppermute | solution.py:29
  531.7 3.5 collective-permute-start.19
  536.5 13.6 %collective-permute-start.21 = (f32[96,512]{1,0:T(8,128)}, f32[96,512]{1,0:T(8,128)}, u32[]{:S(2)}, u32[]{:S(2)}) collective-permute-start(f32[96,512]{1,0:T(8,128)} %broadcast_multiply_fusion.1), channel_id=1, source_target_pairs={{2,0},{3,1},{4,2},{5,3},{6,4},{7,5},{8,6},{9,7},{10,8},{11,9},{12,... | collective-permute-start | bytes 589832 | tf_op jit(solution)/shard_map/ppermute | solution.py:29
  538.5 12.4 %collective-permute-start.20 = (f32[96,512]{1,0:T(8,128)}, f32[96,512]{1,0:T(8,128)}, u32[]{:S(2)}, u32[]{:S(2)}) collective-permute-start(f32[96,512]{1,0:T(8,128)} %broadcast_multiply_fusion.1), channel_id=1, source_target_pairs={{0,2},{1,3},{2,4},{3,5},{4,6},{5,7},{6,8},{7,9},{8,10},{9,11},{10,... | collective-permute-start | bytes 589832 | tf_op jit(solution)/shard_map/ppermute | solution.py:29
  557.2 25.3 %copy-start.40 = (s32[96]{0:T(128)S(1)}, s32[96]{0:T(128)}, u32[]{:S(2)}) copy-start(s32[96]{0:T(128)} %param.21) | copy-start | bytes 1156
  565.8 4.9 collective-permute-start.22
  573.1 12.6 %collective-permute-start.24 = (f32[96,512]{1,0:T(8,128)}, f32[96,512]{1,0:T(8,128)}, u32[]{:S(2)}, u32[]{:S(2)}) collective-permute-start(f32[96,512]{1,0:T(8,128)} %multiply_add_fusion.1), channel_id=1, source_target_pairs={{2,0},{3,1},{4,2},{5,3},{6,4},{7,5},{8,6},{9,7},{10,8},{11,9},{12,... | collective-permute-start | bytes 589832 | tf_op jit(solution)/shard_map/ppermute | solution.py:29
  575.0 11.2 %collective-permute-start.23 = (f32[96,512]{1,0:T(8,128)}, f32[96,512]{1,0:T(8,128)}, u32[]{:S(2)}, u32[]{:S(2)}) collective-permute-start(f32[96,512]{1,0:T(8,128)} %multiply_add_fusion.1), channel_id=1, source_target_pairs={{0,2},{1,3},{2,4},{3,5},{4,6},{5,7},{6,8},{7,9},{8,10},{9,11},{10,... | collective-permute-start | bytes 589832 | tf_op jit(solution)/shard_map/ppermute | solution.py:29
  598.9 4.0 collective-permute-start.25
  605.0 12.6 %copy-start.14 = (f32[96,512]{1,0:T(8,128)S(1)}, f32[96,512]{1,0:T(8,128)}, u32[]{:S(2)}) copy-start(f32[96,512]{1,0:T(8,128)} %copy-done.12) | copy-start | bytes 589828
  606.1 26.1 %copy-start.1 = (f32[96,64,64]{2,1,0:T(8,128)S(1)}, f32[96,64,64]{2,1,0:T(8,128)}, u32[]{:S(2)}) copy-start(f32[96,64,64]{2,1,0:T(8,128)} %copy-done) | copy-start | bytes 4718596
  620.5 18.5 %collective-permute-start.27 = (f32[96,512]{1,0:T(8,128)}, f32[96,512]{1,0:T(8,128)}, u32[]{:S(2)}, u32[]{:S(2)}) collective-permute-start(f32[96,512]{1,0:T(8,128)} %add_add_fusion.1), channel_id=1, source_target_pairs={{1,0},{2,1},{3,2},{4,3},{5,4},{6,5},{7,6},{8,7},{9,8},{10,9},{11,1... | collective-permute-start | bytes 589832 | tf_op jit(solution)/shard_map/ppermute | solution.py:42
  622.7 17.9 %collective-permute-start.26 = (f32[96,512]{1,0:T(8,128)}, f32[96,512]{1,0:T(8,128)}, u32[]{:S(2)}, u32[]{:S(2)}) collective-permute-start(f32[96,512]{1,0:T(8,128)} %add_add_fusion.1), channel_id=1, source_target_pairs={{0,1},{1,2},{2,3},{3,4},{4,5},{5,6},{6,7},{7,8},{8,9},{9,10},{10,1... | collective-permute-start | bytes 589832 | tf_op jit(solution)/shard_map/ppermute | solution.py:40
  647.5 12.5 %copy-start.15 = (f32[96,512]{1,0:T(8,128)S(1)}, f32[96,512]{1,0:T(8,128)}, u32[]{:S(2)}) copy-start(f32[96,512]{1,0:T(8,128)} %param.15) | copy-start | bytes 589828
  662.8 17.1 %collective-permute-start.29 = (f32[96,512]{1,0:T(8,128)}, f32[96,512]{1,0:T(8,128)}, u32[]{:S(2)}, u32[]{:S(2)}) collective-permute-start(f32[96,512]{1,0:T(8,128)} %get-tuple-element.4), channel_id=1, source_target_pairs={{1,0},{2,1},{3,2},{4,3},{5,4},{6,5},{7,6},{8,7},{9,8},{10,9},{11,1... | collective-permute-start | bytes 589832 | tf_op jit(solution)/shard_map/ppermute | solution.py:42
  664.7 16.8 %collective-permute-start.28 = (f32[96,512]{1,0:T(8,128)}, f32[96,512]{1,0:T(8,128)}, u32[]{:S(2)}, u32[]{:S(2)}) collective-permute-start(f32[96,512]{1,0:T(8,128)} %get-tuple-element.4), channel_id=1, source_target_pairs={{0,1},{1,2},{2,3},{3,4},{4,5},{5,6},{6,7},{7,8},{8,9},{9,10},{10,1... | collective-permute-start | bytes 589832 | tf_op jit(solution)/shard_map/ppermute | solution.py:40
  701.8 18.1 %collective-permute-start.31 = (f32[96,512]{1,0:T(8,128)S(1)}, f32[96,512]{1,0:T(8,128)}, u32[]{:S(2)}, u32[]{:S(2)}) collective-permute-start(f32[96,512]{1,0:T(8,128)S(1)} %get-tuple-element.2), channel_id=1, source_target_pairs={{1,0},{2,1},{3,2},{4,3},{5,4},{6,5},{7,6},{8,7},{9,8},{10,9},{11,1... | collective-permute-start | bytes 589832 | tf_op jit(solution)/shard_map/ppermute | solution.py:42
  703.7 17.9 %collective-permute-start.30 = (f32[96,512]{1,0:T(8,128)S(1)}, f32[96,512]{1,0:T(8,128)}, u32[]{:S(2)}, u32[]{:S(2)}) collective-permute-start(f32[96,512]{1,0:T(8,128)S(1)} %get-tuple-element.2), channel_id=1, source_target_pairs={{0,1},{1,2},{2,3},{3,4},{4,5},{5,6},{6,7},{7,8},{8,9},{9,10},{10,1... | collective-permute-start | bytes 589832 | tf_op jit(solution)/shard_map/ppermute | solution.py:40
  719.8 4.3 copy-start.21
  724.2 7.5 %copy-start.16 = (f32[96,512]{1,0:T(8,128)S(1)}, f32[96,512]{1,0:T(8,128)}, u32[]{:S(2)}) copy-start(f32[96,512]{1,0:T(8,128)} %add_add_fusion.1) | copy-start | bytes 589828
  724.2 7.5 %copy-start.19 = (f32[96,512]{1,0:T(8,128)S(1)}, f32[96,512]{1,0:T(8,128)}, u32[]{:S(2)}) copy-start(f32[96,512]{1,0:T(8,128)} %get-tuple-element.5) | copy-start | bytes 589828
  724.2 7.5 %copy-start.29 = (f32[96,512]{1,0:T(8,128)S(1)}, f32[96,512]{1,0:T(8,128)}, u32[]{:S(2)}) copy-start(f32[96,512]{1,0:T(8,128)} %get-tuple-element.3) | copy-start | bytes 589828
  (10 other events, 30.9 us)
Sparse Core Ops, SparseCore 0:
  279.1 119.8 all-reduce.1
where the time goes:
time: 748 us; the launch traced here: 740 us
  matrix products  209 us (28%)
  local copies, waits for them, and re-layouts  206 us (28%)
  waiting for transfers between devices  145 us (19%)
  starting transfers between devices  118 us (16%)
  other arithmetic  47.3 us (6%)
  between operations  15.2 us (2%)
    psum x1, waiting for transfers between devices, body(): lax.psum(restrict(prol_two, agg_two, own_residual, COARSE), ('grp', 'dev'))  113 us
    dot_general x19, matrix products, apply_tiles(): jnp.einsum('ikab,ikvb->iva', as_tiles(offd_part), picked, precision=highest)  102 us
    dot_general x19, matrix products, apply_tiles(): jnp.einsum('iab,ivb->iva', as_tiles(diag_part), own_rows, precision=highest)  84.9 us
    ppermute x12, starting transfers between devices, shifted(): lax.ppermute(value, axis, [(source, source + steps) for source in range(i...  54.1 us
    ppermute x6, starting transfers between devices, padded_2(): lax.ppermute(tail, axis, [(i, (i + 1) % count) for i in range(ends)])  45.7 us
    reshape x8, local copies, waits for them, and re-layouts, as_tiles(): return flat_tile.reshape(flat_tile.shape[:-1] + (TILE, TILE))  31.6 us
    reshape x19, local copies, waits for them, and re-layouts, apply_tiles(): picked = picked.reshape(picked.shape[0], picked.shape[1], LOADS, TILE)  29.9 us
    ppermute x8, waiting for transfers between devices, partner(): return lax.ppermute(value, axis, pairs)  23.6 us
  transfers between devices with their start and end apart: 33, of which 16 were waited for; matrix products, arithmetic and copies ran while one was open for 16% of the time, Pallas kernels for 0%

commit v1 on v0

v1 whole, which is shorter than its diff:
```python
import functools

import jax
import jax.numpy as jnp
from jax import lax
from jax.experimental import pallas as pl
from jax.experimental.pallas import tpu as pltpu
from jax.sharding import PartitionSpec as P

MESH = pl.DeviceIdType.MESH
TILE = 64
LOADS = 8
ROWS = 96
HALF = 48
COARSE = 32
GHOST = 24
UNROLL = 8
CENTER = 5.0
RADIUS = 4.0
F32 = jnp.float32
BF16 = jnp.bfloat16


def chebyshev_steps(degree):
    sigma = CENTER / RADIUS
    rho, pairs = 1.0 / sigma, []
    for _ in range(degree - 1):
        rho_next = 1.0 / (2.0 * sigma - rho)
        pairs.append((rho_next * rho, 2.0 * rho_next / RADIUS))
        rho = rho_next
    return pairs


STEPS = chebyshev_steps(3)
COARSE_STEPS = chebyshev_steps(8)


def halves(u):
    high = u.astype(BF16).astype(F32)
    return jnp.concatenate([high, u - high], 0).astype(BF16)


def twice(out):
    total = out[:LOADS] + out[LOADS:]
    return jnp.concatenate([total, total], 1)


def apply_one(u, tile):
    return twice(
        lax.dot_general(halves(u), tile, (((1,), (1,)), ((), ())), preferred_element_type=F32)
    )


def apply_two(u, w, tiles):
    left = jnp.concatenate([halves(u), halves(w)], 1)
    return twice(
        lax.dot_general(left, tiles, (((1,), (1,)), ((), ())), preferred_element_type=F32)
    )


def apply_transposed(u, tile):
    out = lax.dot_general(
        halves(u)[:, :TILE], tile, (((1,), (0,)), ((), ())), preferred_element_type=F32
    )
    total = out[:LOADS] + out[LOADS:]
    return total + pltpu.roll(total, TILE, 1)


def rows_loop(count, compute, store):
    def step(turn, carry):
        base = turn * UNROLL
        results = [compute(base + j) for j in range(UNROLL)]
        for j in range(UNROLL):
            store(base + j, results[j])
        return carry

    lax.fori_loop(0, count // UNROLL, step, 0)


def kernel(
    groups,
    size,
    rhs_ref,
    to_left_ref,
    to_right_ref,
    cols_one,
    diag_one,
    offd_one,
    prol_one,
    agg_one,
    hot_one,
    cols_two,
    diag_two,
    offd_two,
    prol_two,
    agg_two,
    hot_two,
    cols_three,
    diag_three,
    offd_three,
    out_ref,
    coarse_ref,
    win_one,
    send_one,
    got_one,
    x_one,
    r_one,
    win_two,
    send_two,
    got_two,
    x_two,
    r_two,
    rhs_two,
    terms,
    part,
    half_in,
    pair_send,
    pair_in,
    pair_all,
    terms_two,
    coarse_part,
    gather_a,
    gather_b,
    total_c,
    full_c,
    d_three,
    r_three,
    send_sem_one,
    recv_sem_one,
    send_sem_two,
    recv_sem_two,
    half_sem,
    pair_sem,
    sem_a,
    sem_b,
    sem_c,
):
    g, e = lax.axis_index("grp"), lax.axis_index("dev")
    me = g * size + e
    last = groups * size - 1
    pair, h = me // 2, me % 2
    pairs = groups * size // 2
    has_left, has_right = me > 0, me < last
    has_prev, has_next = pair > 0, pair < pairs - 1
    share = COARSE // size

    def at(index):
        return (index // size, index % size)

    lanes = lax.broadcasted_iota(jnp.int32, (LOADS, 2 * TILE), 1)
    low = lanes < TILE

    def unpack(packed):
        turned = pltpu.roll(packed, TILE, 1)
        return jnp.where(low, packed, turned), jnp.where(low, turned, packed)

    barrier = pltpu.get_barrier_semaphore()

    def greet(device):
        pl.semaphore_signal(barrier, inc=1, device_id=device, device_id_type=MESH)

    for k in range(1, size):
        greet((g, (e + k) % size))
    for k in range(1, groups):
        greet(((g + k) % groups, e))

    @pl.when(has_left)
    def _():
        greet(at(me - 1))

    @pl.when(has_right)
    def _():
        greet(at(me + 1))

    @pl.when(has_prev)
    def _():
        greet(at(2 * pair - 2))
        greet(at(2 * pair - 1))

    @pl.when(has_next)
    def _():
        greet(at(2 * pair + 2))
        greet(at(2 * pair + 3))

    def one(flag):
        return flag.astype(jnp.int32)

    expected = size - 1 + groups - 1 + one(has_left) + one(has_right)
    pl.semaphore_wait(barrier, expected + 2 * one(has_prev) + 2 * one(has_next))

    def level_one(s, store):
        def copy(side):
            target = at(me - 1) if side == 0 else at(me + 1)
            return pltpu.make_async_remote_copy(
                src_ref=send_one.at[s, side],
                dst_ref=got_one.at[s, 1 - side],
                send_sem=send_sem_one.at[s, side],
                recv_sem=recv_sem_one.at[s, 1 - side],
                device_id=target,
                device_id_type=MESH,
            )

        flags = (has_left, has_right)
        for side, rows in ((0, to_left_ref), (1, to_right_ref)):

            @pl.when(flags[side])
            def _(side=side, rows=rows):
                for t in range(GHOST // 2):
                    first = win_one[s, GHOST + rows[t]]
                    second = win_one[s, GHOST + rows[t + GHOST // 2]]
                    send_one[s, side, t] = jnp.where(low, first, second)
                copy(side).start()

        def diag(i):
            return r_one[i] - apply_one(win_one[s, GHOST + i], diag_one[i])

        def keep(i, value):
            r_one[i] = value

        rows_loop(ROWS, diag, keep)
        for side in range(2):
            base = 0 if side == 0 else GHOST + ROWS

            @pl.when(flags[side])
            def _(side=side, base=base):
                copy(1 - side).wait_recv()
                copy(side).wait_send()
                for t in range(GHOST // 2):
                    first, second = unpack(got_one[s, side, t])
                    win_one[s, base + t] = first
                    win_one[s, base + t + GHOST // 2] = second

            @pl.when(jnp.logical_not(flags[side]))
            def _(base=base):
                win_one[s, base : base + GHOST] = jnp.zeros((GHOST, LOADS, 2 * TILE), F32)

        def offd(i):
            return r_one[i] - apply_two(
                win_one[s, cols_one[i, 0]], win_one[s, cols_one[i, 1]], offd_one[i]
            )

        rows_loop(ROWS, offd, store)

    def level_two(s, store):
        own = ROWS + HALF * h

        def copy(target, slot):
            return pltpu.make_async_remote_copy(
                src_ref=send_two.at[s],
                dst_ref=got_two.at[s, slot],
                send_sem=send_sem_two.at[s, target_index[0]],
                recv_sem=recv_sem_two.at[s, slot],
                device_id=at(target),
                device_id_type=MESH,
            )

        target_index = [0]

        def make(number, target, slot):
            target_index[0] = number
            return copy(target, slot)

        for t in range(HALF // 2):
            send_two[s, t] = jnp.where(
                low, win_two[s, own + t], win_two[s, own + t + HALF // 2]
            )

        def prev_copies():
            return [make(y, 2 * pair - 2 + y, 3 + h) for y in range(2)]

        def next_copies():
            return [make(3 + y, 2 * pair + 2 + y, h) for y in range(2)]

        def partner_copy():
            return make(2, me + 1 - 2 * h, 2)

        @pl.when(has_prev)
        def _():
            for c in prev_copies():
                c.start()

        @pl.when(has_next)
        def _():
            for c in next_copies():
                c.start()

        partner_copy().start()

        def diag(j):
            return r_two[j] - apply_one(win_two[s, own + j], diag_two[j])

        def keep(j, value):
            r_two[j] = value

        rows_loop(HALF, diag, keep)

        def take(slot, base):
            for t in range(HALF // 2):
                first, second = unpack(got_two[s, slot, t])
                win_two[s, base + t] = first
                win_two[s, base + t + HALF // 2] = second

        partner_copy().wait()
        take(2, ROWS + HALF * (1 - h))

        @pl.when(has_prev)
        def _():
            for y, c in enumerate(prev_copies()):
                c.wait_send()
                make(y, 2 * pair - 2 + y, y).wait_recv()
                take(y, HALF * y)

        @pl.when(jnp.logical_not(has_prev))
        def _():
            win_two[s, 0:ROWS] = jnp.zeros((ROWS, LOADS, 2 * TILE), F32)

        @pl.when(has_next)
        def _():
            for y, c in enumerate(next_copies()):
                c.wait_send()
                make(3 + y, 2 * pair + 2 + y, 3 + y).wait_recv()
                take(3 + y, 2 * ROWS + HALF * y)

        @pl.when(jnp.logical_not(has_next))
        def _():
            win_two[s, 2 * ROWS : 3 * ROWS] = jnp.zeros((ROWS, LOADS, 2 * TILE), F32)

        def offd(j):
            return r_two[j] - apply_two(
                win_two[s, cols_two[j, 0]], win_two[s, cols_two[j, 1]], offd_two[j]
            )

        rows_loop(HALF, offd, store)

    for i in range(ROWS):
        value = rhs_ref[i]
        r_one[i] = value
        win_one[0, GHOST + i] = value / CENTER
        x_one[i] = value / CENTER

    def smooth_one(s, step):
        old, new = STEPS[step]

        def store(i, value):
            r_one[i] = value
            turn = old * win_one[s, GHOST + i] + new * value
            win_one[s + 1, GHOST + i] = turn
            x_one[i] = x_one[i] + turn

        level_one(s, store)

    def keep_one(i, value):
        r_one[i] = value

    smooth_one(0, 0)
    smooth_one(1, 1)
    level_one(2, keep_one)

    def restrict_one(i, value):
        terms[pl.ds(pl.multiple_of(i * LOADS, LOADS), LOADS), :] = value

    rows_loop(ROWS, lambda i: apply_transposed(r_one[i], prol_one[i]), restrict_one)

    def gathered(hot_ref, terms_ref, part_ref, count, fine):
        hot = hot_ref[...]
        wide = lax.broadcasted_iota(jnp.int32, (fine, 2 * TILE), 1) < TILE
        for v in range(LOADS):
            value = terms_ref[pl.ds(v, fine, stride=LOADS), :]
            high = value.astype(BF16).astype(F32)
            mixed = jnp.where(wide, high, value - high).astype(BF16)
            out = jnp.dot(hot, mixed, preferred_element_type=F32)
            part_ref[pl.ds(v, count, stride=LOADS), :] = out + pltpu.roll(out, TILE, 1)

    gathered(hot_one, terms, part, ROWS, ROWS)

    partner = at(me + 1 - 2 * h)
    mine, theirs = HALF * LOADS * h, HALF * LOADS * (1 - h)

    def part_rows(base, j):
        return part[pl.ds(pl.multiple_of(base + j * LOADS, LOADS), LOADS), :]

    for t in range(HALF // 2):
        pair_send[0, t] = jnp.where(
            low, part_rows(theirs, t), part_rows(theirs, t + HALF // 2)
        )
    half_copy = pltpu.make_async_remote_copy(
        src_ref=pair_send.at[0],
        dst_ref=half_in,
        send_sem=half_sem.at[0],
        recv_sem=half_sem.at[1],
        device_id=partner,
        device_id_type=MESH,
    )
    half_copy.start()
    half_copy.wait()
    own = ROWS + HALF * h
    for t in range(HALF // 2):
        for j, other in zip((t, t + HALF // 2), unpack(half_in[t])):
            value = part_rows(mine, j) + other
            rhs_two[j] = value
            r_two[j] = value
            win_two[0, own + j] = value / CENTER
            x_two[j] = value / CENTER

    def smooth_two(s, step):
        old, new = STEPS[step]

        def store(j, value):
            r_two[j] = value
            turn = old * win_two[s, own + j] + new * value
            x_two[j] = x_two[j] + turn
            win_two[s + 1, own + j] = turn

        level_two(s, store)

    def keep_two(j, value):
        r_two[j] = value

    smooth_two(0, 0)
    smooth_two(1, 1)
    level_two(2, keep_two)

    def restrict_two(j, value):
        terms_two[pl.ds(pl.multiple_of(j * LOADS, LOADS), LOADS), :] = value

    rows_loop(HALF, lambda j: apply_transposed(r_two[j], prol_two[j]), restrict_two)
    gathered(hot_two, terms_two, coarse_part, COARSE, HALF)

    width = share * LOADS

    def rows_of(member):
        return pl.ds(pl.multiple_of(member * width, LOADS), width)

    def copy_a(k):
        target = (e + k) % size
        return pltpu.make_async_remote_copy(
            src_ref=coarse_part.at[rows_of(target)],
            dst_ref=gather_a.at[k],
            send_sem=sem_a.at[0, k],
            recv_sem=sem_a.at[1, k],
            device_id=(g, target),
            device_id_type=MESH,
        )

    for k in range(1, size):
        copy_a(k).start()
    total = coarse_part[rows_of(e), :]
    for k in range(1, size):
        copy_a(k).wait()
        total = total + gather_a[k]
    gather_b[g] = total

    def copy_b(k, member):
        return pltpu.make_async_remote_copy(
            src_ref=gather_b.at[g],
            dst_ref=gather_b.at[member],
            send_sem=sem_b.at[0, k],
            recv_sem=sem_b.at[1, k],
            device_id=((g + k) % groups, e),
            device_id_type=MESH,
        )

    for k in range(1, groups):
        copy_b(k, g).start()
    for k in range(1, groups):
        copy_b(k, g).wait_send()
        copy_b(k, (g + groups - k) % groups).wait_recv()
    total = gather_b[0]
    for k in range(1, groups):
        total = total + gather_b[k]
    full_c[rows_of(e), :] = total

    def copy_c(k, member):
        return pltpu.make_async_remote_copy(
            src_ref=full_c.at[rows_of(e)],
            dst_ref=full_c.at[rows_of(member)],
            send_sem=sem_c.at[0, k],
            recv_sem=sem_c.at[1, k],
            device_id=(g, (e + k) % size),
            device_id_type=MESH,
        )

    for k in range(1, size):
        copy_c(k, e).start()
    for k in range(1, size):
        copy_c(k, e).wait_send()
        copy_c(k, (e + size - k) % size).wait_recv()

    for c in range(COARSE):
        value = full_c[c * LOADS : (c + 1) * LOADS, :]
        r_three[c] = value
        d_three[0, c] = value / CENTER
        coarse_ref[c] = value / CENTER

    for s, (old, new) in enumerate(COARSE_STEPS):
        now, later = s % 2, 1 - s % 2

        def coarse(c, now=now):
            return (
                r_three[c]
                - apply_one(d_three[now, c], diag_three[c])
                - apply_two(
                    d_three[now, cols_three[c, 0]],
                    d_three[now, cols_three[c, 1]],
                    offd_three[c],
                )
            )

        def store(c, value, now=now, later=later, old=old, new=new):
            r_three[c] = value
            turn = old * d_three[now, c] + new * value
            d_three[later, c] = turn
            coarse_ref[c] = coarse_ref[c] + turn

        rows_loop(COARSE, coarse, store)

    def corrected_two(j):
        return x_two[j] + apply_one(coarse_ref[agg_two[j]], prol_two[j])

    def store_two(j, value):
        x_two[j] = value
        r_two[j] = rhs_two[j]
        win_two[3, own + j] = value

    rows_loop(HALF, corrected_two, store_two)

    def first_two(j, value):
        r_two[j] = value
        turn = value / CENTER
        win_two[4, own + j] = turn
        x_two[j] = x_two[j] + turn

    level_two(3, first_two)
    smooth_two(4, 0)

    def last_two(j, value):
        turn = STEPS[1][0] * win_two[5, own + j] + STEPS[1][1] * value
        pair_all[HALF * h + j] = x_two[j] + turn

    level_two(5, last_two)
    for t in range(HALF // 2):
        pair_send[1, t] = jnp.where(
            low, pair_all[HALF * h + t], pair_all[HALF * h + t + HALF // 2]
        )
    pair_copy = pltpu.make_async_remote_copy(
        src_ref=pair_send.at[1],
        dst_ref=pair_in,
        send_sem=pair_sem.at[0],
        recv_sem=pair_sem.at[1],
        device_id=partner,
        device_id_type=MESH,
    )
    pair_copy.start()
    pair_copy.wait()
    for t in range(HALF // 2):
        first, second = unpack(pair_in[t])
        pair_all[HALF * (1 - h) + t] = first
        pair_all[HALF * (1 - h) + t + HALF // 2] = second

    def corrected_one(i):
        return x_one[i] + apply_one(pair_all[agg_one[i]], prol_one[i])

    def store_one(i, value):
        x_one[i] = value
        r_one[i] = rhs_ref[i]
        win_one[3, GHOST + i] = value

    rows_loop(ROWS, corrected_one, store_one)

    def first_one(i, value):
        r_one[i] = value
        turn = value / CENTER
        win_one[4, GHOST + i] = turn
        x_one[i] = x_one[i] + turn

    level_one(3, first_one)
    smooth_one(4, 0)

    def last_one(i, value):
        turn = STEPS[1][0] * win_one[5, GHOST + i] + STEPS[1][1] * value
        out_ref[i] = x_one[i] + turn

    level_one(5, last_one)


def split(tiles):
    high = lax.reduce_precision(tiles, 8, 7)
    return jnp.concatenate([high.astype(BF16), (tiles - high).astype(BF16)], -1)


def single(flat):
    return split(flat.reshape(flat.shape[0], TILE, TILE))


def double(flat):
    tiles = flat.reshape(flat.shape[0], 2, TILE, TILE)
    return jnp.concatenate([split(tiles[:, 0]), split(tiles[:, 1])], -1)


def body(
    groups,
    size,
    right_side,
    ghost_rows,
    cols_one,
    diag_one,
    offd_one,
    prol_one,
    agg_one,
    cols_two,
    diag_two,
    offd_two,
    prol_two,
    agg_two,
    cols_three,
    diag_three,
    offd_three,
):
    count = groups * size
    axes = ("grp", "dev")
    to_right = lax.ppermute(ghost_rows[0], axes, [(i + 1, i) for i in range(count - 1)])
    to_left = lax.ppermute(ghost_rows[1], axes, [(i, i + 1) for i in range(count - 1)])
    rhs = right_side.reshape(ROWS, LOADS, TILE)
    rhs = jnp.concatenate([rhs, rhs], -1)
    hot_one = (agg_one[None, :] == jnp.arange(ROWS, dtype=jnp.int32)[:, None]).astype(BF16)
    hot_two = (agg_two[None, :] == jnp.arange(COARSE, dtype=jnp.int32)[:, None]).astype(BF16)
    smem = pl.BlockSpec(memory_space=pltpu.SMEM)
    vmem = pl.BlockSpec(memory_space=pltpu.VMEM)
    row = (LOADS, 2 * TILE)
    share = COARSE // size
    dma = pltpu.SemaphoreType.DMA
    out, coarse = pl.pallas_call(
        functools.partial(kernel, groups, size),
        out_shape=(
            jax.ShapeDtypeStruct((ROWS, *row), F32),
            jax.ShapeDtypeStruct((COARSE, *row), F32),
        ),
        in_specs=[vmem, smem, smem]
        + [smem, vmem, vmem, vmem, smem, vmem] * 2
        + [smem, vmem, vmem],
        out_specs=(vmem, vmem),
        scratch_shapes=[
            pltpu.VMEM((6, ROWS + 2 * GHOST, *row), F32),
            pltpu.VMEM((6, 2, GHOST // 2, *row), F32),
            pltpu.VMEM((6, 2, GHOST // 2, *row), F32),
            pltpu.VMEM((ROWS, *row), F32),
            pltpu.VMEM((ROWS, *row), F32),
            pltpu.VMEM((6, 3 * ROWS, *row), F32),
            pltpu.VMEM((6, HALF // 2, *row), F32),
            pltpu.VMEM((6, 5, HALF // 2, *row), F32),
            pltpu.VMEM((HALF, *row), F32),
            pltpu.VMEM((HALF, *row), F32),
            pltpu.VMEM((HALF, *row), F32),
            pltpu.VMEM((ROWS * LOADS, 2 * TILE), F32),
            pltpu.VMEM((ROWS * LOADS, 2 * TILE), F32),
            pltpu.VMEM((HALF // 2, *row), F32),
            pltpu.VMEM((2, HALF // 2, *row), F32),
            pltpu.VMEM((HALF // 2, *row), F32),
            pltpu.VMEM((ROWS, *row), F32),
            pltpu.VMEM((HALF * LOADS, 2 * TILE), F32),
            pltpu.VMEM((COARSE * LOADS, 2 * TILE), F32),
            pltpu.VMEM((size, share * LOADS, 2 * TILE), F32),
            pltpu.VMEM((groups, share * LOADS, 2 * TILE), F32),
            pltpu.VMEM((share * LOADS, 2 * TILE), F32),
            pltpu.VMEM((COARSE * LOADS, 2 * TILE), F32),
            pltpu.VMEM((2, COARSE, *row), F32),
            pltpu.VMEM((COARSE, *row), F32),
            dma((6, 2)),
            dma((6, 2)),
            dma((6, 5)),
            dma((6, 5)),
            dma((2,)),
            dma((2,)),
            dma((2, size)),
            dma((2, groups)),
            dma((2, size)),
        ],
        compiler_params=pltpu.CompilerParams(
            collective_id=0, has_side_effects=True, vmem_limit_bytes=56 * 2**20
        ),
    )(
        rhs,
        to_left,
        to_right,
        cols_one,
        single(diag_one),
        double(offd_one),
        single(prol_one),
        agg_one,
        hot_one,
        cols_two,
        single(diag_two),
        double(offd_two),
        single(prol_two),
        agg_two,
        hot_two,
        cols_three,
        single(diag_three),
        double(offd_three),
    )
    return (
        out[:, :, :TILE].reshape(ROWS, LOADS * TILE),
        coarse[:, :, :TILE].reshape(COARSE, LOADS * TILE),
    )


def solution(mesh):
    groups, size = mesh.shape["grp"], mesh.shape["dev"]
    rows = P(("grp", "dev"), None)
    tiles = P(("grp", "dev"), None, None)
    flat = P(("grp", "dev"))
    return jax.shard_map(
        functools.partial(body, groups, size),
        mesh=mesh,
        in_specs=(
            rows,
            rows,
            rows,
            rows,
            tiles,
            rows,
            flat,
            rows,
            rows,
            tiles,
            rows,
            flat,
            P(),
            P(),
            P(),
        ),
        out_specs=(rows, P()),
        check_vma=False,
    )
```

time: 748 us -> 264 us (0.35); the launches traced: 740 us -> 263 us
  matrix products: 209 us -> 0 us
  Pallas kernels: 0 us -> 164 us
  local copies, waits for them, and re-layouts: 206 us -> 58.4 us
  waiting for transfers between devices: 145 us -> 0.01 us
  starting transfers between devices: 118 us -> 5.27 us
  between operations: 15.2 us -> 0.94 us
  other arithmetic: 47.3 us -> 34.8 us
    dot_general x44 -> x0, matrix products: 209 us -> none  [the longest x19 102 us: apply_tiles(): jnp.einsum('ikab,ikvb->iva', as_tiles(offd_part), picked, precision=highest)]
    pallas_call x0 -> x1, Pallas kernels: none -> 164 us  [body(): pl.pallas_call(functools.partial(kernel, groups, size), out_shape=(jax.Sh...]
    psum x1 -> x0, waiting for transfers between devices: 113 us -> none  [body(): lax.psum(restrict(prol_two, agg_two, own_residual, COARSE), ('grp', 'dev'))]
    ppermute x32 -> x2, starting transfers between devices: 118 us -> 5.27 us  [the longest x1 3.27 us: body(): lax.ppermute(ghost_rows[1], axes, [(i, i + 1) for i in range(count - 1)])]
    reshape x72 -> x9, local copies, waits for them, and re-layouts: 111 us -> 16.2 us  [the longest x5 10 us: single(): return split(flat.reshape(flat.shape[0], TILE, TILE))]
    gather x34 -> x0, local copies, waits for them, and re-layouts: 54.9 us -> none  [the longest x6 14.4 us: pair_reader(): return jnp.concatenate([left_pair, vector, right_pair], 0)[cols]]
    ppermute x32 -> x2, waiting for transfers between devices: 31.1 us -> 0.01 us  [the longest x1 0.01 us: body(): lax.ppermute(ghost_rows[1], axes, [(i, i + 1) for i in range(count - 1)])]
    add x17 -> x0, other arithmetic: 22.6 us -> none  [the longest x12 15.9 us: chebyshev(): rho_next * rho_now * direction + 2.0 * rho_next / radius * residual]
  transfers between devices with their start and end apart: 33 -> 2, of which waited for: 16 -> 0; matrix products, arithmetic and copies ran while one was open for 16% -> 32% of each run, Pallas kernels for 0% -> 0%
where the time goes in v1:
time: 264 us; the launch traced here: 263 us
  Pallas kernels  164 us (62%)
  local copies, waits for them, and re-layouts  58.4 us (22%)
  other arithmetic  34.8 us (13%)
  starting transfers between devices  5.27 us (2%)
    pallas_call x1, Pallas kernels, body(): pl.pallas_call(functools.partial(kernel, groups, size), out_shape=(jax.Sh...  164 us
    unnamed x74, local copies, waits for them, and re-layouts  27.3 us
    convert_element_type x8, other arithmetic, split(): return jnp.concatenate([high.astype(BF16), (tiles - high).astype(BF16)], -1)  15.5 us
    reshape x5, local copies, waits for them, and re-layouts, single(): return split(flat.reshape(flat.shape[0], TILE, TILE))  10 us
    reduce_precision x2, local copies, waits for them, and re-layouts, split(): high = lax.reduce_precision(tiles, 8, 7)  8.48 us
    concatenate x3, other arithmetic, double(): return jnp.concatenate([split(tiles[:, 0]), split(tiles[:, 1])], -1)  7.56 us
    concatenate x3, other arithmetic, split(): return jnp.concatenate([high.astype(BF16), (tiles - high).astype(BF16)], -1)  6.51 us
  transfers between devices with their start and end apart: 2, of which 0 were waited for; matrix products, arithmetic and copies ran while one was open for 32% of the time, Pallas kernels for 0%

profile of v1, /device:TPU:29, one launch (start us, length us, event | category | flops | bytes accessed | tf_op | source)
XLA Modules:
  0.0 263.4 jit_solution(13028063352353315724)
XLA Ops:
  0.6 1.4 slice_bitcast_fusion.4
  2.0 3.3 %collective-permute-start = (s32[24]{0:T(128)}, s32[24]{0:T(128)}, u32[]{:S(2)}, u32[]{:S(2)}) collective-permute-start(s32[24]{0:T(128)} %get-tuple-element.35), channel_id=1, source_target_pairs={{0,1},{1,2},{2,3},{3,4},{4,5},{5,6},{6,7},{7,8},{8,9},{9,10},{10,1... | collective-permute-start | bytes 296 | tf_op jit(solution)/shard_map/ppermute | solution.py:622
  5.3 2.0 collective-permute-start.1
  7.3 1.8 copy.52
  9.1 1.5 reduce_precision.36
  10.6 3.7 %copy.54 = f32[96,64,64]{2,1,0:T(8,128)} copy(f32[96,64,64]{0,2,1:T(8,128)S(1)} %bitcast.46) | data formatting | bytes 3145728 | tf_op jit(solution)/shard_map/reshape | solution.py:592
  14.3 1.8 copy.45
  16.2 1.5 reduce_precision.33
  17.7 3.7 %copy.47 = f32[96,64,64]{2,1,0:T(8,128)} copy(f32[96,64,64]{0,2,1:T(8,128)S(1)} %bitcast.48) | data formatting | bytes 3145728 | tf_op jit(solution)/shard_map/reshape | solution.py:592
  21.3 5.9 %copy.49 = f32[96,2,4096]{0,2,1:T(8,128)} copy(f32[96,2,4096]{2,1,0:T(2,128)} %param.19) | data formatting | bytes 6291456 | tf_op args[4]
  27.3 4.0 %fusion.11 = (f32[96,1,64,64]{0,3,2,1:T(8,128)S(1)}, f32[96,1,64,64]{0,3,2,1:T(8,128)}) fusion(f32[96,2,64,64]{0,3,2,1:T(8,128)} %bitcast.49), kind=kLoop, calls=%fused_computation.48 | loop fusion | bytes 6291456 | tf_op jit(solution)/shard_map/slice | solution.py:597
  31.2 3.6 %copy.63 = f32[96,1,64,64]{3,2,0,1:T(8,128)} copy(f32[96,1,64,64]{0,3,2,1:T(8,128)S(1)} %get-tuple-element.10) | data formatting | bytes 3145728
  34.9 4.9 %copy.64 = f32[96,1,64,64]{3,2,0,1:T(8,128)} copy(f32[96,1,64,64]{0,3,2,1:T(8,128)} %get-tuple-element.11) | data formatting | bytes 3145728
  39.7 0.0 copy-done.5
  39.7 3.6 %copy.53 = f32[96,64,64]{2,1,0:T(8,128)} copy(f32[96,64,64]{0,2,1:T(8,128)S(1)} %copy-done.5) | data formatting | bytes 3145728 | tf_op jit(solution)/shard_map/reduce_precision | solution.py:587
  43.4 4.8 %copy.46 = f32[96,64,64]{2,1,0:T(8,128)} copy(f32[96,64,64]{0,2,1:T(8,128)} %reduce_precision.33) | data formatting | bytes 3145728 | tf_op jit(solution)/shard_map/reduce_precision | solution.py:587
  48.2 0.0 copy-done.20
  48.2 2.1 copy.56
  50.3 2.6 reshape.44
  52.9 0.0 copy-start.21
  52.9 2.4 reduce-precision_convert_fusion.4
  55.3 0.6 copy.57
  55.9 0.8 reshape.47
  56.7 0.0 copy-start.22
  56.7 1.7 reduce-precision_convert_fusion.7
  58.5 0.6 reshape.45
  59.1 0.0 copy-start.23
  59.1 1.6 reduce-precision_convert_fusion.2
  60.8 0.6 reshape.43
  61.4 0.0 copy-start.24
  61.4 1.6 reduce-precision_convert_fusion.5
  63.0 1.4 reshape.46
  64.4 2.7 %reduce-precision_convert_fusion.8 = (bf16[32,64,64]{2,1,0:T(8,128)(2,1)}, bf16[32,64,64]{2,1,0:T(8,128)(2,1)}) fusion(f32[32,64,64]{2,1,0:T(8,128)} %reshape.46), kind=kLoop, calls=%fused_computation.31 | loop fusion | flops 524288 | bytes 1048576 | tf_op jit(solution)/shard_map/convert_element_type | solution.py:588
  67.1 0.9 copy.42
  67.9 1.1 copy.43
  69.1 0.9 pad_maximum_fusion.8.rhs_ref
  70.0 0.0 copy-done.28
  70.0 0.7 copy.58.cols_one
  70.7 0.7 copy.59.cols_two
  71.4 0.6 fusion.9.hot_one
  72.1 0.6 fusion.10.hot_two
  72.7 0.0 copy-done.4
  72.7 3.8 %reduce-precision_convert_fusion = (bf16[96,64,64]{2,1,0:T(8,128)(2,1)S(1)}, bf16[96,64,64]{2,1,0:T(8,128)(2,1)S(1)}, bf16[96,64,64]{2,1,0:T(8,128)(2,1)S(1)}, bf16[96,64,64]{2,1,0:T(8,128)(2,1)S(1)}) fusion(f32[96,1,64,64]{3,2,0,1:T(8,128)} %copy.64, f32[96,1,64,64]{3,2,0,1:T(8,128)S(1)} %copy-done.4), kind=kLoop, calls=%fused_computation.1 | loop fusion | flops 3145728 | bytes 6291456 | tf_op jit(solution)/shard_map/convert_element_type | solution.py:588
  76.5 0.9 fusion.12
  77.4 1.0 copy-done
  78.4 1.0 copy-done.2
  79.3 0.9 fusion.13
  80.2 0.2 copy-done.14
  80.4 0.2 copy-done.15
  80.5 1.1 pad_maximum_fusion.7.diag_three
  81.6 3.5 %pad_maximum_fusion.offd_one = bf16[96,64,256]{2,1,0:T(8,128)(2,1)} fusion(bf16[96,64,64]{2,1,0:T(8,128)(2,1)S(1)} %get-tuple-element.21, bf16[96,64,64]{2,1,0:T(8,128)(2,1)S(1)} %get-tuple-element.20, bf16[96,64,64]{2,1,0:T(8,128)(2,1)S(1)} %get-tuple-element.36, bf16[96,64,64]{2,1,0:T(8,128)(2,1)S(1)} %get-tuple-element.37), kind=kLoop, calls=%fused_computation.6 | loop fusion | flops 12582912 | bytes 6291456 | tf_op jit(solution)/shard_map/concatenate | solution.py:597
  85.2 3.4 %pad_maximum_fusion.1 = (bf16[96,64,128]{2,1,0:T(8,128)(2,1)}, bf16[96,64,128]{2,1,0:T(8,128)(2,1)}) fusion(bf16[96,64,64]{2,1,0:T(8,128)(2,1)S(1)} %get-tuple-element.23, bf16[96,64,64]{2,1,0:T(8,128)(2,1)S(1)} %get-tuple-element.22, bf16[96,64,64]{2,1,0:T(8,128)(2,1)S(1)} %get-tuple-element.17, bf16[96,64,64]{2,1,0:T(8,128)(2,1)S(1)} %get-tuple-element.16), kind=kLoop, calls=%fused_computation.23 | loop fusion | flops 6291456 | bytes 6291456 | tf_op jit(solution)/shard_map/concatenate | solution.py:588
  88.6 2.2 pad_maximum_fusion.3.offd_two
  90.9 1.8 pad_maximum_fusion.4.offd_three
  92.7 0.0 copy-done.10
  92.7 0.4 copy-done.13
  93.1 2.0 pad_maximum_fusion.5
  95.1 0.7 copy.60.cols_three
  95.8 0.0 collective-permute-done.to_left_ref
  95.8 0.0 collective-permute-done.1.to_right_ref
  95.8 164.0 %shard_map.158 = (f32[96,8,128]{2,1,0:T(8,128)}, f32[32,8,128]{2,1,0:T(8,128)}) custom-call(f32[96,8,128]{2,1,0:T(8,128)} %pad_maximum_fusion.8.rhs_ref, s32[24]{0:T(128)} %collective-permute-done.to_left_ref, s32[24]{0:T(128)} %collective-permute-done.1.to_right_ref, s32[96,2]{1,0:T(8,128)} %copy.58.cols_one, ...), custom_call_target="tpu_custom_call" | custom-call | tf_op jit(solution)/shard_map/pallas_call | solution.py:632
  259.8 1.1 copy.61
  260.9 0.8 copy.62
  261.7 1.6 reshape.49
  (48 shorter events, 0.1 us)
Async XLA Ops:
  2.0 93.8 %collective-permute-start = (s32[24]{0:T(128)}, s32[24]{0:T(128)}, u32[]{:S(2)}, u32[]{:S(2)}) collective-permute-start(s32[24]{0:T(128)} %get-tuple-element.35), channel_id=1, source_target_pairs={{0,1},{1,2},{2,3},{3,4},{4,5},{5,6},{6,7},{7,8},{8,9},{9,10},{10,1... | collective-permute-start | bytes 296 | tf_op jit(solution)/shard_map/ppermute | solution.py:622
  5.3 90.6 %collective-permute-start.1 = (s32[24]{0:T(128)}, s32[24]{0:T(128)}, u32[]{:S(2)}, u32[]{:S(2)}) collective-permute-start(s32[24]{0:T(128)} %get-tuple-element.34), channel_id=1, source_target_pairs={{1,0},{2,1},{3,2},{4,3},{5,4},{6,5},{7,6},{8,7},{9,8},{10,9},{11,1... | collective-permute-start | bytes 296 | tf_op jit(solution)/shard_map/ppermute | solution.py:621
  34.9 4.9 %copy-start.5 = (f32[96,64,64]{0,2,1:T(8,128)S(1)}, f32[96,64,64]{0,2,1:T(8,128)}, u32[]{:S(2)}) copy-start(f32[96,64,64]{0,2,1:T(8,128)} %reduce_precision.36) | copy-start | bytes 4718596
  43.4 4.8 %copy-start.20 = (f32[48,2,4096]{2,1,0:T(2,128)S(1)}, f32[48,2,4096]{2,1,0:T(2,128)}, u32[]{:S(2)}) copy-start(f32[48,2,4096]{2,1,0:T(2,128)} %param.24) | copy-start | bytes 4718596
  52.9 2.4 copy-start.21
  56.7 1.8 copy-start.22
  59.1 1.6 copy-start.23
  61.4 1.6 copy-start.24
  63.0 4.1 %copy-start.25 = (f32[96,512]{1,0:T(8,128)S(1)}, f32[96,512]{1,0:T(8,128)}, u32[]{:S(2)}) copy-start(f32[96,512]{1,0:T(8,128)} %param.15) | copy-start | bytes 589828
  64.4 5.6 %copy-start.28 = (s32[96,2]{0,1:T(2,128)S(1)}, s32[96,2]{0,1:T(2,128)}, u32[]{:S(2)}) copy-start(s32[96,2]{0,1:T(2,128)} %param.17) | copy-start | bytes 2308
  64.4 6.4 %copy-start.29 = (s32[48,2]{0,1:T(2,128)S(1)}, s32[48,2]{0,1:T(2,128)}, u32[]{:S(2)}) copy-start(s32[48,2]{0,1:T(2,128)} %param.22) | copy-start | bytes 1156
  64.4 7.1 %copy-start.26 = (s32[96]{0:T(128)S(1)}, s32[96]{0:T(128)}, u32[]{:S(2)}) copy-start(s32[96]{0:T(128)} %agg_one.1) | copy-start | bytes 1156
  64.4 7.7 %copy-start.27 = (s32[48]{0:T(128)S(1)}, s32[48]{0:T(128)}, u32[]{:S(2)}) copy-start(s32[48]{0:T(128)} %agg_two.1) | copy-start | bytes 580
  64.4 8.3 %copy-start.4 = (f32[96,1,64,64]{3,2,0,1:T(8,128)S(1)}, f32[96,1,64,64]{3,2,0,1:T(8,128)}, u32[]{:S(2)}) copy-start(f32[96,1,64,64]{3,2,0,1:T(8,128)} %copy.63) | copy-start | bytes 4718596
  72.7 3.8 %copy-start.1 = (f32[96,64,64]{2,1,0:T(8,128)S(1)}, f32[96,64,64]{2,1,0:T(8,128)}, u32[]{:S(2)}) copy-start(f32[96,64,64]{2,1,0:T(8,128)} %copy.54) | copy-start | bytes 4718596
  72.7 3.8 %copy-start.3 = (f32[96,64,64]{2,1,0:T(8,128)S(1)}, f32[96,64,64]{2,1,0:T(8,128)}, u32[]{:S(2)}) copy-start(f32[96,64,64]{2,1,0:T(8,128)} %copy.53) | copy-start | bytes 4718596
  76.5 1.9 copy-start
  76.5 2.8 %copy-start.2 = (f32[96,64,64]{2,1,0:T(8,128)S(1)}, f32[96,64,64]{2,1,0:T(8,128)}, u32[]{:S(2)}) copy-start(f32[96,64,64]{2,1,0:T(8,128)} %copy.46) | copy-start | bytes 4718596
  79.3 1.0 copy-start.14
  79.3 1.2 copy-start.15
  85.2 3.4 %copy-start.6 = (bf16[48,64,64]{2,1,0:T(8,128)(2,1)S(1)}, bf16[48,64,64]{2,1,0:T(8,128)(2,1)}, u32[]{:S(2)}) copy-start(bf16[48,64,64]{2,1,0:T(8,128)(2,1)} %get-tuple-element.12) | copy-start | bytes 1179652
  85.2 3.4 %copy-start.7 = (bf16[48,64,64]{2,1,0:T(8,128)(2,1)S(1)}, bf16[48,64,64]{2,1,0:T(8,128)(2,1)}, u32[]{:S(2)}) copy-start(bf16[48,64,64]{2,1,0:T(8,128)(2,1)} %get-tuple-element.13) | copy-start | bytes 1179652
  85.2 3.4 %copy-start.8 = (bf16[48,64,64]{2,1,0:T(8,128)(2,1)S(1)}, bf16[48,64,64]{2,1,0:T(8,128)(2,1)}, u32[]{:S(2)}) copy-start(bf16[48,64,64]{2,1,0:T(8,128)(2,1)} %get-tuple-element.14) | copy-start | bytes 1179652
  85.2 3.4 %copy-start.9 = (bf16[48,64,64]{2,1,0:T(8,128)(2,1)S(1)}, bf16[48,64,64]{2,1,0:T(8,128)(2,1)}, u32[]{:S(2)}) copy-start(bf16[48,64,64]{2,1,0:T(8,128)(2,1)} %get-tuple-element.15) | copy-start | bytes 1179652
  88.6 2.3 copy-start.16
  88.6 2.3 copy-start.17
  88.6 2.3 copy-start.18
  88.6 2.3 copy-start.19
  90.9 1.8 copy-start.10
  90.9 1.8 copy-start.11
  90.9 1.8 copy-start.12
  90.9 2.2 copy-start.13
  93.1 2.0 copy-start.30

commit v2 on v1

--- a/solution.py
+++ b/solution.py
@@ -2,6 +2,7 @@
 
 import jax
 import jax.numpy as jnp
+import numpy as np
 from jax import lax
 from jax.experimental import pallas as pl
 from jax.experimental.pallas import tpu as pltpu
@@ -14,7 +15,8 @@
 HALF = 48
 COARSE = 32
 GHOST = 24
-UNROLL = 8
+UNROLL = 24
+GROUP = 8
 CENTER = 5.0
 RADIUS = 4.0
 F32 = jnp.float32
@@ -31,6 +33,23 @@
     return pairs
 
 
+def spread():
+    order = np.concatenate([np.arange(0, TILE, 2), np.arange(1, TILE, 2)])
+    move = np.zeros((TILE, TILE), np.float32)
+    move[order, np.arange(TILE)] = 1.0
+    tiles = np.zeros((2, 2, TILE, 2, 2, TILE), np.float32)
+    for part in range(2):
+        for parity in range(2):
+            tiles[part, parity, :, parity, part, :] = move
+    enter = np.zeros((2, 2, TILE, 2, TILE), np.float32)
+    leave = np.zeros((2, TILE, 2, TILE), np.float32)
+    for half in range(2):
+        enter[half, half, :, 0] = enter[half, half, :, 1] = move
+        leave[half, :, half] = move.T
+    rows = np.concatenate([enter.reshape(4 * TILE, -1), leave.reshape(2 * TILE, -1)])
+    return tiles.reshape(4 * TILE, 4 * TILE), rows.reshape(3, 2 * TILE, 2 * TILE)
+
+
 STEPS = chebyshev_steps(3)
 COARSE_STEPS = chebyshev_steps(8)
 
@@ -66,75 +85,163 @@
     return total + pltpu.roll(total, TILE, 1)
 
 
-def rows_loop(count, compute, store):
+def rows_loop(count, compute, store, unroll=UNROLL):
     def step(turn, carry):
-        base = turn * UNROLL
-        results = [compute(base + j) for j in range(UNROLL)]
-        for j in range(UNROLL):
+        base = turn * unroll
+        results = [compute(base + j) for j in range(unroll)]
+        for j in range(unroll):
             store(base + j, results[j])
         return carry
 
-    lax.fori_loop(0, count // UNROLL, step, 0)
+    lax.fori_loop(0, count // unroll, step, 0)
+
+
+def exact_dot(value, matrix):
+    high = value.astype(BF16)
+    rest = value - high.astype(F32)
+    middle = rest.astype(BF16)
+    small = (rest - middle.astype(F32)).astype(BF16)
+    first, second, third = (
+        jnp.dot(part, matrix, preferred_element_type=F32) for part in (high, middle, small)
+    )
+    return first + second + third
+
+
+def converted(tiles, matrix):
+    value = jnp.concatenate(tiles, 0)
+    high = value.astype(BF16)
+    small = (value - high.astype(F32)).astype(BF16)
+    both = jnp.concatenate([high, small], 1)
+    return jnp.dot(both, matrix, preferred_element_type=F32).astype(BF16)
+
+
+def keep_tile(ref, i, lanes, rows):
+    ref[i, : TILE // 2, lanes] = rows[:, : 2 * TILE]
+    ref[i, TILE // 2 :, lanes] = rows[:, 2 * TILE :]
+
+
+def convert_single(raw, ref, matrix, count):
+    def step(turn, carry):
+        base = pl.multiple_of(turn * GROUP * TILE // 2, GROUP * TILE // 2)
+        tiles = [raw[pl.ds(base + j, TILE // 2, stride=GROUP), :] for j in range(GROUP)]
+        out = converted(tiles, matrix[...])
+        for j in range(GROUP):
+            rows = out[j * TILE // 2 : (j + 1) * TILE // 2]
+            keep_tile(ref, turn * GROUP + j, slice(0, 2 * TILE), rows)
+        return carry
+
+    lax.fori_loop(0, count // GROUP, step, 0)
+
+
+def convert_double(raw, ref, matrix, count):
+    def step(turn, carry):
+        base = pl.multiple_of(turn * GROUP * TILE // 2, GROUP * TILE // 2)
+        tiles = [
+            raw[pl.ds(base + j * TILE + k, TILE // 2, stride=2), :]
+            for j in range(GROUP // 2)
+            for k in range(2)
+        ]
+        out = converted(tiles, matrix[...])
+        for j in range(GROUP // 2):
+            for k in range(2):
+                place = 2 * j + k
+                rows = out[place * TILE // 2 : (place + 1) * TILE // 2]
+                lanes = slice(2 * TILE * k, 2 * TILE * (k + 1))
+                keep_tile(ref, turn * (GROUP // 2) + j, lanes, rows)
+        return carry
+
+    lax.fori_loop(0, count // (GROUP // 2), step, 0)
 
 
 def kernel(
     groups,
     size,
-    rhs_ref,
-    to_left_ref,
-    to_right_ref,
+    matrix,
+    moves,
+    rhs_in,
+    ghost_rows,
     cols_one,
-    diag_one,
-    offd_one,
-    prol_one,
+    diag_one_raw,
+    offd_one_raw,
+    prol_one_raw,
     agg_one,
     hot_one,
     cols_two,
-    diag_two,
-    offd_two,
-    prol_two,
+    diag_two_raw,
+    offd_two_raw,
+    prol_two_raw,
     agg_two,
     hot_two,
     cols_three,
-    diag_three,
-    offd_three,
+    diag_three_raw,
+    offd_three_raw,
     out_ref,
-    coarse_ref,
-    win_one,
-    send_one,
-    got_one,
-    x_one,
-    r_one,
-    win_two,
-    send_two,
-    got_two,
-    x_two,
-    r_two,
-    rhs_two,
-    terms,
-    part,
-    half_in,
-    pair_send,
-    pair_in,
-    pair_all,
-    terms_two,
-    coarse_part,
-    gather_a,
-    gather_b,
-    total_c,
-    full_c,
-    d_three,
-    r_three,
-    send_sem_one,
-    recv_sem_one,
-    send_sem_two,
-    recv_sem_two,
-    half_sem,
-    pair_sem,
-    sem_a,
-    sem_b,
-    sem_c,
+    coarse_out,
+    *scratch,
 ):
+    raws = (
+        diag_one_raw,
+        offd_one_raw,
+        prol_one_raw,
+        diag_two_raw,
+        offd_two_raw,
+        prol_two_raw,
+        diag_three_raw,
+        offd_three_raw,
+    )
+    staged, tiles, scratch = scratch[:8], scratch[8:16], scratch[16:]
+    diag_one, offd_one, prol_one, diag_two, offd_two, prol_two, diag_three, offd_three = tiles
+    (
+        rhs_one,
+        win_one,
+        send_one,
+        got_one,
+        x_one,
+        r_one,
+        win_two,
+        send_two,
+        got_two,
+        x_two,
+        r_two,
+        rhs_two,
+        terms,
+        part,
+        half_in,
+        pair_send,
+        pair_in,
+        pair_all,
+        terms_two,
+        coarse_part,
+        gather_a,
+        gather_b,
+        full_c,
+        d_three,
+        r_three,
+        coarse_ref,
+        lists_in,
+        lists,
+        stage_sem,
+        list_sem,
+        send_sem_one,
+        recv_sem_one,
+        send_sem_two,
+        recv_sem_two,
+        half_sem,
+        pair_sem,
+        sem_a,
+        sem_b,
+        sem_c,
+    ) = scratch
+    stages = [
+        pltpu.make_async_copy(raws[k], staged[k], stage_sem.at[k]) for k in range(8)
+    ]
+    for stage in stages:
+        stage.start()
+
+    def prepare(k, convert, count):
+        stages[k].wait()
+        convert(staged[k], tiles[k], matrix, count)
+
     g, e = lax.axis_index("grp"), lax.axis_index("dev")
     me = g * size + e
     last = groups * size - 1
@@ -188,7 +295,43 @@
     expected = size - 1 + groups - 1 + one(has_left) + one(has_right)
     pl.semaphore_wait(barrier, expected + 2 * one(has_prev) + 2 * one(has_next))
 
-    def level_one(s, store):
+    def list_copy(side):
+        return pltpu.make_async_remote_copy(
+            src_ref=ghost_rows,
+            dst_ref=lists_in.at[1 - side],
+            send_sem=list_sem.at[0, side],
+            recv_sem=list_sem.at[1, 1 - side],
+            device_id=at(me - 1) if side == 0 else at(me + 1),
+            device_id_type=MESH,
+        )
+
+    for side, flag in ((0, has_left), (1, has_right)):
+
+        @pl.when(flag)
+        def _(side=side):
+            list_copy(side).start()
+
+    for q in range(LOADS // 2):
+        value = rhs_in[:, 2 * TILE * q : 2 * TILE * (q + 1)]
+        for half in range(2):
+            rhs_one[pl.ds(2 * q + half, ROWS, stride=LOADS), :] = exact_dot(value, moves[half])
+
+    def rhs_row(i):
+        return rhs_one[pl.ds(pl.multiple_of(i * LOADS, LOADS), LOADS), :]
+
+    for side, flag in ((0, has_left), (1, has_right)):
+
+        @pl.when(flag)
+        def _(side=side):
+            list_copy(1 - side).wait_recv()
+            list_copy(side).wait_send()
+            local = pltpu.make_async_copy(
+                lists_in.at[side], lists.at[side], list_sem.at[2, side]
+            )
+            local.start()
+            local.wait()
+
+    def level_one(s, store, before=None, during=None):
         def copy(side):
             target = at(me - 1) if side == 0 else at(me + 1)
             return pltpu.make_async_remote_copy(
@@ -201,16 +344,19 @@
             )
 
         flags = (has_left, has_right)
-        for side, rows in ((0, to_left_ref), (1, to_right_ref)):
+        for side in range(2):
 
             @pl.when(flags[side])
-            def _(side=side, rows=rows):
+            def _(side=side):
                 for t in range(GHOST // 2):
-                    first = win_one[s, GHOST + rows[t]]
-                    second = win_one[s, GHOST + rows[t + GHOST // 2]]
+                    first = win_one[s, GHOST + lists[side, 1 - side, t]]
+                    second = win_one[s, GHOST + lists[side, 1 - side, t + GHOST // 2]]
                     send_one[s, side, t] = jnp.where(low, first, second)
                 copy(side).start()
 
+        if before:
+            before()
+
         def diag(i):
             return r_one[i] - apply_one(win_one[s, GHOST + i], diag_one[i])
 
@@ -218,6 +364,8 @@
             r_one[i] = value
 
         rows_loop(ROWS, diag, keep)
+        if during:
+            during()
         for side in range(2):
             base = 0 if side == 0 else GHOST + ROWS
 
@@ -241,7 +389,7 @@
 
         rows_loop(ROWS, offd, store)
 
-    def level_two(s, store):
+    def level_two(s, store, during=None):
         own = ROWS + HALF * h
 
         def copy(target, slot):
@@ -293,6 +441,8 @@
             r_two[j] = value
 
         rows_loop(HALF, diag, keep)
+        if during:
+            during()
 
         def take(slot, base):
             for t in range(HALF // 2):
@@ -333,12 +483,12 @@
         rows_loop(HALF, offd, store)
 
     for i in range(ROWS):
-        value = rhs_ref[i]
+        value = rhs_row(i)
         r_one[i] = value
         win_one[0, GHOST + i] = value / CENTER
         x_one[i] = value / CENTER
 
-    def smooth_one(s, step):
+    def smooth_one(s, step, before=None, during=None):
         old, new = STEPS[step]
 
         def store(i, value):
@@ -347,14 +497,23 @@
             win_one[s + 1, GHOST + i] = turn
             x_one[i] = x_one[i] + turn
 
-        level_one(s, store)
+        level_one(s, store, before, during)
 
     def keep_one(i, value):
         r_one[i] = value
 
-    smooth_one(0, 0)
-    smooth_one(1, 1)
-    level_one(2, keep_one)
+    def prepare_prol_one():
+        prepare(2, convert_single, ROWS)
+        prepare(3, convert_single, HALF)
+
+    smooth_one(
+        0,
+        0,
+        lambda: prepare(0, convert_single, ROWS),
+        lambda: prepare(1, convert_double, ROWS),
+    )
+    smooth_one(1, 1, None, prepare_prol_one)
+    level_one(2, keep_one, None, lambda: prepare(4, convert_double, HALF))
 
     def restrict_one(i, value):
         terms[pl.ds(pl.multiple_of(i * LOADS, LOADS), LOADS), :] = value
@@ -402,7 +561,7 @@
             win_two[0, own + j] = value / CENTER
             x_two[j] = value / CENTER
 
-    def smooth_two(s, step):
+    def smooth_two(s, step, during=None):
         old, new = STEPS[step]
 
         def store(j, value):
@@ -411,14 +570,14 @@
             x_two[j] = x_two[j] + turn
             win_two[s + 1, own + j] = turn
 
-        level_two(s, store)
+        level_two(s, store, during)
 
     def keep_two(j, value):
         r_two[j] = value
 
-    smooth_two(0, 0)
-    smooth_two(1, 1)
-    level_two(2, keep_two)
+    smooth_two(0, 0, lambda: prepare(5, convert_single, HALF))
+    smooth_two(1, 1, lambda: prepare(6, convert_single, COARSE))
+    level_two(2, keep_two, lambda: prepare(7, convert_double, COARSE))
 
     def restrict_two(j, value):
         terms_two[pl.ds(pl.multiple_of(j * LOADS, LOADS), LOADS), :] = value
@@ -512,7 +671,7 @@
             d_three[later, c] = turn
             coarse_ref[c] = coarse_ref[c] + turn
 
-        rows_loop(COARSE, coarse, store)
+        rows_loop(COARSE, coarse, store, 16)
 
     def corrected_two(j):
         return x_two[j] + apply_one(coarse_ref[agg_two[j]], prol_two[j])
@@ -562,7 +721,7 @@
 
     def store_one(i, value):
         x_one[i] = value
-        r_one[i] = rhs_ref[i]
+        r_one[i] = rhs_row(i)
         win_one[3, GHOST + i] = value
 
     rows_loop(ROWS, corrected_one, store_one)
@@ -578,23 +737,35 @@
 
     def last_one(i, value):
         turn = STEPS[1][0] * win_one[5, GHOST + i] + STEPS[1][1] * value
-        out_ref[i] = x_one[i] + turn
+        terms[pl.ds(pl.multiple_of(i * LOADS, LOADS), LOADS), :] = x_one[i] + turn
 
     level_one(5, last_one)
 
-
-def split(tiles):
-    high = lax.reduce_precision(tiles, 8, 7)
-    return jnp.concatenate([high.astype(BF16), (tiles - high).astype(BF16)], -1)
+    def leave(stage_ref, target_ref, count):
+        wide = lax.broadcasted_iota(jnp.int32, (count, 2 * TILE), 1) < TILE
+        for q in range(LOADS // 2):
+            first = stage_ref[pl.ds(2 * q, count, stride=LOADS), :]
+            second = stage_ref[pl.ds(2 * q + 1, count, stride=LOADS), :]
+            target_ref[:, 2 * TILE * q : 2 * TILE * (q + 1)] = exact_dot(
+                jnp.where(wide, first, second), moves[2]
+            )
+
+    leave(terms, out_ref, ROWS)
+    for c in range(COARSE):
+        coarse_part[c * LOADS : (c + 1) * LOADS, :] = coarse_ref[c]
+    leave(coarse_part, coarse_out, COARSE)
 
 
 def single(flat):
-    return split(flat.reshape(flat.shape[0], TILE, TILE))
+    count = flat.shape[0]
+    tiles = flat.reshape(count // GROUP, GROUP, TILE // 2, 2 * TILE)
+    return tiles.transpose(0, 2, 1, 3).reshape(count * TILE // 2, 2 * TILE)
 
 
 def double(flat):
-    tiles = flat.reshape(flat.shape[0], 2, TILE, TILE)
-    return jnp.concatenate([split(tiles[:, 0]), split(tiles[:, 1])], -1)
+    count = flat.shape[0]
+    tiles = flat.reshape(count, 2, TILE // 2, 2 * TILE)
+    return tiles.transpose(0, 2, 1, 3).reshape(count * TILE, 2 * TILE)
 
 
 def body(
@@ -616,12 +787,7 @@
     diag_three,
     offd_three,
 ):
-    count = groups * size
-    axes = ("grp", "dev")
-    to_right = lax.ppermute(ghost_rows[0], axes, [(i + 1, i) for i in range(count - 1)])
-    to_left = lax.ppermute(ghost_rows[1], axes, [(i, i + 1) for i in range(count - 1)])
-    rhs = right_side.reshape(ROWS, LOADS, TILE)
-    rhs = jnp.concatenate([rhs, rhs], -1)
+    matrix, moves = (jnp.asarray(a, BF16) for a in spread())
     hot_one = (agg_one[None, :] == jnp.arange(ROWS, dtype=jnp.int32)[:, None]).astype(BF16)
     hot_two = (agg_two[None, :] == jnp.arange(COARSE, dtype=jnp.int32)[:, None]).astype(BF16)
     smem = pl.BlockSpec(memory_space=pltpu.SMEM)
@@ -629,17 +795,33 @@
     row = (LOADS, 2 * TILE)
     share = COARSE // size
     dma = pltpu.SemaphoreType.DMA
-    out, coarse = pl.pallas_call(
+    hbm = pl.BlockSpec(memory_space=pl.ANY)
+    raw = [
+        single(diag_one),
+        double(offd_one),
+        single(prol_one),
+        single(diag_two),
+        double(offd_two),
+        single(prol_two),
+        single(diag_three),
+        double(offd_three),
+    ]
+    widths = [2, 4, 2, 2, 4, 2, 2, 4]
+    counts = [ROWS] * 3 + [HALF] * 3 + [COARSE] * 2
+    return pl.pallas_call(
         functools.partial(kernel, groups, size),
         out_shape=(
-            jax.ShapeDtypeStruct((ROWS, *row), F32),
-            jax.ShapeDtypeStruct((COARSE, *row), F32),
+            jax.ShapeDtypeStruct((ROWS, LOADS * TILE), F32),
+            jax.ShapeDtypeStruct((COARSE, LOADS * TILE), F32),
         ),
-        in_specs=[vmem, smem, smem]
-        + [smem, vmem, vmem, vmem, smem, vmem] * 2
-        + [smem, vmem, vmem],
+        in_specs=[vmem] * 4
+        + [smem, hbm, hbm, hbm, smem, vmem] * 2
+        + [smem, hbm, hbm],
         out_specs=(vmem, vmem),
-        scratch_shapes=[
+        scratch_shapes=[pltpu.VMEM(a.shape, F32) for a in raw]
+        + [pltpu.VMEM((n, TILE, w * TILE), BF16) for n, w in zip(counts, widths)]
+        + [
+            pltpu.VMEM((ROWS * LOADS, 2 * TILE), F32),
             pltpu.VMEM((6, ROWS + 2 * GHOST, *row), F32),
             pltpu.VMEM((6, 2, GHOST // 2, *row), F32),
             pltpu.VMEM((6, 2, GHOST // 2, *row), F32),
@@ -661,10 +843,14 @@
             pltpu.VMEM((COARSE * LOADS, 2 * TILE), F32),
             pltpu.VMEM((size, share * LOADS, 2 * TILE), F32),
             pltpu.VMEM((groups, share * LOADS, 2 * TILE), F32),
-            pltpu.VMEM((share * LOADS, 2 * TILE), F32),
             pltpu.VMEM((COARSE * LOADS, 2 * TILE), F32),
             pltpu.VMEM((2, COARSE, *row), F32),
             pltpu.VMEM((COARSE, *row), F32),
+            pltpu.VMEM((COARSE, *row), F32),
+            pltpu.VMEM((2, 2, GHOST), jnp.int32),
+            pltpu.SMEM((2, 2, GHOST), jnp.int32),
+            dma((8,)),
+            dma((3, 2)),
             dma((6, 2)),
             dma((6, 2)),
             dma((6, 5)),
@@ -679,28 +865,20 @@
             collective_id=0, has_side_effects=True, vmem_limit_bytes=56 * 2**20
         ),
     )(
-        rhs,
-        to_left,
-        to_right,
+        matrix,
+        moves,
+        right_side,
+        ghost_rows,
         cols_one,
-        single(diag_one),
-        double(offd_one),
-        single(prol_one),
+        *raw[:3],
         agg_one,
         hot_one,
         cols_two,
-        single(diag_two),
-        double(offd_two),
-        single(prol_two),
+        *raw[3:6],
         agg_two,
         hot_two,
         cols_three,
-        single(diag_three),
-        double(offd_three),
-    )
-    return (
-        out[:, :, :TILE].reshape(ROWS, LOADS * TILE),
-        coarse[:, :, :TILE].reshape(COARSE, LOADS * TILE),
+        *raw[6:],
     )
 
 

time: 264 us -> 161 us (0.61)
  local copies, waits for them, and re-layouts: 58.4 us -> 7.21 us
  other arithmetic: 34.8 us -> 2.53 us
  Pallas kernels: 164 us -> 150 us
  starting transfers between devices: 5.27 us -> 0 us
    unnamed x74 -> x5, local copies, waits for them, and re-layouts: 27.3 us -> 7.21 us
    reshape x9 -> x0, local copies, waits for them, and re-layouts: 16.2 us -> none  [the longest x5 10 us: single(): return split(flat.reshape(flat.shape[0], TILE, TILE))]
    convert_element_type x8 -> x0, other arithmetic: 15.5 us -> none  [split(): return jnp.concatenate([high.astype(BF16), (tiles - high).astype(BF16)], -1)]
    concatenate x7 -> x0, other arithmetic: 15 us -> none  [the longest x3 7.56 us: double(): return jnp.concatenate([split(tiles[:, 0]), split(tiles[:, 1])], -1)]
    pallas_call x1, Pallas kernels: 164 us -> 150 us  [body(): pl.pallas_call(functools.partial(kernel, groups, size), out_shape=(jax.Sh...]
    reduce_precision x2 -> x0, local copies, waits for them, and re-layouts: 8.48 us -> none  [split(): high = lax.reduce_precision(tiles, 8, 7)]
    ppermute x2 -> x0, starting transfers between devices: 5.27 us -> none  [the longest x1 3.27 us: body(): lax.ppermute(ghost_rows[1], axes, [(i, i + 1) for i in range(count - 1)])]
    slice x2 -> x0, local copies, waits for them, and re-layouts: 5.13 us -> none  [the longest x1 3.98 us: double(): return jnp.concatenate([split(tiles[:, 0]), split(tiles[:, 1])], -1)]
  transfers between devices with their start and end apart: 2 -> 0, of which waited for: 0 -> 0; matrix products, arithmetic and copies ran while one was open for 32% -> 0% of each run, Pallas kernels for 0% -> 0%
where the time goes in v2:
time: 161 us
  Pallas kernels  150 us (93%)
  local copies, waits for them, and re-layouts  7.21 us (4%)
  other arithmetic  2.53 us (2%)
    pallas_call x1, Pallas kernels, body(): pl.pallas_call(functools.partial(kernel, groups, size), out_shape=(jax.Sh...  150 us
    unnamed x5, local copies, waits for them, and re-layouts  7.21 us

profile of v2, /device:TPU:29, one launch (start us, length us, event | category | flops | bytes accessed | tf_op | source)
XLA Modules:
  0.0 160.6 jit_solution(9417933067655146420)
XLA Ops:
  0.6 1.3 fusion.1.hot_two
  1.9 1.4 copy.24.cols_three
  3.2 1.4 copy.23.cols_two
  4.6 1.3 fusion.hot_one
  5.9 1.4 copy.22.cols_one
  7.3 150.2 %shard_map.176 = (f32[96,512]{1,0:T(8,128)}, f32[32,512]{1,0:T(8,128)}) custom-call(bf16[256,256]{1,0:T(8,128)(2,1)} %constant.4.clone.matrix, bf16[3,128,128]{2,1,0:T(8,128)(2,1)} %constant.5.clone.moves, f32[96,512]{1,0:T(8,128)} %rhs_in.1, s32[2,24]{1,0:T(2,128)} %ghost_rows.1, s32[96,2]{1,0:T(8,128)} %copy.22.cols_one, f32[3072,128]{1,0:T(8,128)} %bitcast.41, ...), custom_call_target="tpu_custom_call" | custom-call | tf_op jit(solution)/shard_map/pallas_call | solution.py:811
  157.5 1.6 %copy.27 = f32[96,512]{1,0:T(8,128)} copy(f32[96,512]{1,0:T(8,128)} %get-tuple-element.4) | data formatting | bytes 393216
  159.1 1.5 copy.28

commit v3 on v2

--- a/solution.py
+++ b/solution.py
@@ -167,6 +167,7 @@
     agg_one,
     hot_one,
     cols_two,
+    cols_two_in,
     diag_two_raw,
     offd_two_raw,
     prol_two_raw,
@@ -214,12 +215,15 @@
         coarse_part,
         gather_a,
         gather_b,
+        packed_c,
         full_c,
         d_three,
         r_three,
         coarse_ref,
         lists_in,
         lists,
+        cols_in,
+        cols_near,
         stage_sem,
         list_sem,
         send_sem_one,
@@ -247,6 +251,7 @@
     last = groups * size - 1
     pair, h = me // 2, me % 2
     pairs = groups * size // 2
+    own = HALF + HALF * h
     has_left, has_right = me > 0, me < last
     has_prev, has_next = pair > 0, pair < pairs - 1
     share = COARSE // size
@@ -281,57 +286,68 @@
 
     @pl.when(has_prev)
     def _():
-        greet(at(2 * pair - 2))
-        greet(at(2 * pair - 1))
+        greet(at(me - 2))
 
     @pl.when(has_next)
     def _():
-        greet(at(2 * pair + 2))
-        greet(at(2 * pair + 3))
-
-    def one(flag):
-        return flag.astype(jnp.int32)
-
-    expected = size - 1 + groups - 1 + one(has_left) + one(has_right)
-    pl.semaphore_wait(barrier, expected + 2 * one(has_prev) + 2 * one(has_next))
-
-    def list_copy(side):
-        return pltpu.make_async_remote_copy(
-            src_ref=ghost_rows,
-            dst_ref=lists_in.at[1 - side],
-            send_sem=list_sem.at[0, side],
-            recv_sem=list_sem.at[1, 1 - side],
-            device_id=at(me - 1) if side == 0 else at(me + 1),
-            device_id_type=MESH,
-        )
-
-    for side, flag in ((0, has_left), (1, has_right)):
-
-        @pl.when(flag)
-        def _(side=side):
-            list_copy(side).start()
+        greet(at(me + 2))
 
     for q in range(LOADS // 2):
         value = rhs_in[:, 2 * TILE * q : 2 * TILE * (q + 1)]
         for half in range(2):
             rhs_one[pl.ds(2 * q + half, ROWS, stride=LOADS), :] = exact_dot(value, moves[half])
 
+    prepare(0, convert_single, ROWS)
+
+    def one(flag):
+        return flag.astype(jnp.int32)
+
+    expected = size - 1 + groups - 1 + one(has_left) + one(has_right)
+    pl.semaphore_wait(barrier, expected + one(has_prev) + one(has_next))
+
+    def list_copy(kind, side):
+        step = kind + 1
+        return pltpu.make_async_remote_copy(
+            src_ref=(ghost_rows, cols_two_in)[kind],
+            dst_ref=(lists_in, cols_in)[kind].at[1 - side],
+            send_sem=list_sem.at[0, kind, side],
+            recv_sem=list_sem.at[1, kind, 1 - side],
+            device_id=at(me - step) if side == 0 else at(me + step),
+            device_id_type=MESH,
+        )
+
+    neighbours = ((has_left, has_right), (has_prev, has_next))
+    for kind in range(2):
+        for side in range(2):
+
+            @pl.when(neighbours[kind][side])
+            def _(kind=kind, side=side):
+                list_copy(kind, side).start()
+
+    prepare(1, convert_double, ROWS)
+
+    def take_lists(kind):
+        for side in range(2):
+
+            @pl.when(neighbours[kind][side])
+            def _(side=side):
+                list_copy(kind, 1 - side).wait_recv()
+                list_copy(kind, side).wait_send()
+                local = pltpu.make_async_copy(
+                    (lists_in, cols_in)[kind].at[side],
+                    (lists, cols_near)[kind].at[side],
+                    list_sem.at[2, kind, side],
+                )
+                local.start()
+                local.wait()
+
+    take_lists(0)
+    take_lists(1)
+
     def rhs_row(i):
         return rhs_one[pl.ds(pl.multiple_of(i * LOADS, LOADS), LOADS), :]
 
-    for side, flag in ((0, has_left), (1, has_right)):
-
-        @pl.when(flag)
-        def _(side=side):
-            list_copy(1 - side).wait_recv()
-            list_copy(side).wait_send()
-            local = pltpu.make_async_copy(
-                lists_in.at[side], lists.at[side], list_sem.at[2, side]
-            )
-            local.start()
-            local.wait()
-
-    def level_one(s, store, before=None, during=None):
+    def level_one(s, store, during=None):
         def copy(side):
             target = at(me - 1) if side == 0 else at(me + 1)
             return pltpu.make_async_remote_copy(
@@ -354,9 +370,6 @@
                     send_one[s, side, t] = jnp.where(low, first, second)
                 copy(side).start()
 
-        if before:
-            before()
-
         def diag(i):
             return r_one[i] - apply_one(win_one[s, GHOST + i], diag_one[i])
 
@@ -384,65 +397,31 @@
 
         def offd(i):
             return r_one[i] - apply_two(
-                win_one[s, cols_one[i, 0]], win_one[s, cols_one[i, 1]], offd_one[i]
+                win_one[s, cols_one[0, i]], win_one[s, cols_one[1, i]], offd_one[i]
             )
 
         rows_loop(ROWS, offd, store)
 
     def level_two(s, store, during=None):
-        own = ROWS + HALF * h
-
-        def copy(target, slot):
+        def partner_copy():
             return pltpu.make_async_remote_copy(
-                src_ref=send_two.at[s],
-                dst_ref=got_two.at[s, slot],
-                send_sem=send_sem_two.at[s, target_index[0]],
-                recv_sem=recv_sem_two.at[s, slot],
-                device_id=at(target),
+                src_ref=send_two.at[s, 2],
+                dst_ref=got_two.at[s, 2],
+                send_sem=send_sem_two.at[s, 2],
+                recv_sem=recv_sem_two.at[s, 2],
+                device_id=at(me + 1 - 2 * h),
                 device_id_type=MESH,
             )
 
-        target_index = [0]
-
-        def make(number, target, slot):
-            target_index[0] = number
-            return copy(target, slot)
-
-        for t in range(HALF // 2):
-            send_two[s, t] = jnp.where(
-                low, win_two[s, own + t], win_two[s, own + t + HALF // 2]
+        def pair_copy(side):
+            return pltpu.make_async_remote_copy(
+                src_ref=send_two.at[s, side],
+                dst_ref=got_two.at[s, 1 - side],
+                send_sem=send_sem_two.at[s, side],
+                recv_sem=recv_sem_two.at[s, 1 - side],
+                device_id=at(me - 2) if side == 0 else at(me + 2),
+                device_id_type=MESH,
             )
-
-        def prev_copies():
-            return [make(y, 2 * pair - 2 + y, 3 + h) for y in range(2)]
-
-        def next_copies():
-            return [make(3 + y, 2 * pair + 2 + y, h) for y in range(2)]
-
-        def partner_copy():
-            return make(2, me + 1 - 2 * h, 2)
-
-        @pl.when(has_prev)
-        def _():
-            for c in prev_copies():
-                c.start()
-
-        @pl.when(has_next)
-        def _():
-            for c in next_copies():
-                c.start()
-
-        partner_copy().start()
-
-        def diag(j):
-            return r_two[j] - apply_one(win_two[s, own + j], diag_two[j])
-
-        def keep(j, value):
-            r_two[j] = value
-
-        rows_loop(HALF, diag, keep)
-        if during:
-            during()
 
         def take(slot, base):
             for t in range(HALF // 2):
@@ -450,35 +429,68 @@
                 win_two[s, base + t] = first
                 win_two[s, base + t + HALF // 2] = second
 
+        for t in range(HALF // 2):
+            send_two[s, 2, t] = jnp.where(
+                low, win_two[s, own + t], win_two[s, own + t + HALF // 2]
+            )
+        partner_copy().start()
+
+        def diag(first):
+            def compute(j):
+                return r_two[first + j] - apply_one(
+                    win_two[s, own + first + j], diag_two[first + j]
+                )
+
+            def keep(j, value):
+                r_two[first + j] = value
+
+            rows_loop(HALF // 2, compute, keep)
+
+        diag(0)
         partner_copy().wait()
-        take(2, ROWS + HALF * (1 - h))
-
-        @pl.when(has_prev)
-        def _():
-            for y, c in enumerate(prev_copies()):
-                c.wait_send()
-                make(y, 2 * pair - 2 + y, y).wait_recv()
-                take(y, HALF * y)
-
-        @pl.when(jnp.logical_not(has_prev))
-        def _():
-            win_two[s, 0:ROWS] = jnp.zeros((ROWS, LOADS, 2 * TILE), F32)
-
-        @pl.when(has_next)
-        def _():
-            for y, c in enumerate(next_copies()):
-                c.wait_send()
-                make(3 + y, 2 * pair + 2 + y, 3 + y).wait_recv()
-                take(3 + y, 2 * ROWS + HALF * y)
-
-        @pl.when(jnp.logical_not(has_next))
-        def _():
-            win_two[s, 2 * ROWS : 3 * ROWS] = jnp.zeros((ROWS, LOADS, 2 * TILE), F32)
+        take(2, HALF + HALF * (1 - h))
+        flags = (has_prev, has_next)
+
+        def wanted(side, t):
+            if side == 0:
+                row = jnp.maximum(cols_near[0, 1, t] - 2 * ROWS, 0)
+            else:
+                row = jnp.minimum(cols_near[1, 0, t], ROWS - 1)
+            return win_two[s, HALF + row]
+
+        for side in range(2):
+
+            @pl.when(flags[side])
+            def _(side=side):
+                for t in range(HALF // 2):
+                    send_two[s, side, t] = jnp.where(
+                        low, wanted(side, t), wanted(side, t + HALF // 2)
+                    )
+                pair_copy(side).start()
+
+        diag(HALF // 2)
+        if during:
+            during()
+        for side in range(2):
+            base = 0 if side == 0 else HALF + ROWS
+
+            @pl.when(flags[side])
+            def _(side=side, base=base):
+                pair_copy(1 - side).wait_recv()
+                pair_copy(side).wait_send()
+                take(side, base)
+
+            @pl.when(jnp.logical_not(flags[side]))
+            def _(base=base):
+                win_two[s, base : base + HALF] = jnp.zeros((HALF, LOADS, 2 * TILE), F32)
 
         def offd(j):
-            return r_two[j] - apply_two(
-                win_two[s, cols_two[j, 0]], win_two[s, cols_two[j, 1]], offd_two[j]
+            before, after = cols_two[0, j], cols_two[1, j]
+            before = jnp.where(before < ROWS, j, before - HALF)
+            after = jnp.where(
+                after < 2 * ROWS, jnp.maximum(after, ROWS) - HALF, HALF + ROWS + j
             )
+            return r_two[j] - apply_two(win_two[s, before], win_two[s, after], offd_two[j])
 
         rows_loop(HALF, offd, store)
 
@@ -488,7 +500,7 @@
         win_one[0, GHOST + i] = value / CENTER
         x_one[i] = value / CENTER
 
-    def smooth_one(s, step, before=None, during=None):
+    def smooth_one(s, step, during=None):
         old, new = STEPS[step]
 
         def store(i, value):
@@ -497,23 +509,14 @@
             win_one[s + 1, GHOST + i] = turn
             x_one[i] = x_one[i] + turn
 
-        level_one(s, store, before, during)
+        level_one(s, store, during)
 
     def keep_one(i, value):
         r_one[i] = value
 
-    def prepare_prol_one():
-        prepare(2, convert_single, ROWS)
-        prepare(3, convert_single, HALF)
-
-    smooth_one(
-        0,
-        0,
-        lambda: prepare(0, convert_single, ROWS),
-        lambda: prepare(1, convert_double, ROWS),
-    )
-    smooth_one(1, 1, None, prepare_prol_one)
-    level_one(2, keep_one, None, lambda: prepare(4, convert_double, HALF))
+    smooth_one(0, 0, lambda: prepare(2, convert_single, ROWS))
+    smooth_one(1, 1, lambda: prepare(3, convert_single, HALF))
+    level_one(2, keep_one, lambda: prepare(4, convert_double, HALF))
 
     def restrict_one(i, value):
         terms[pl.ds(pl.multiple_of(i * LOADS, LOADS), LOADS), :] = value
@@ -521,7 +524,8 @@
     rows_loop(ROWS, lambda i: apply_transposed(r_one[i], prol_one[i]), restrict_one)
 
     def gathered(hot_ref, terms_ref, part_ref, count, fine):
-        hot = hot_ref[...]
+        row = lax.broadcasted_iota(jnp.int32, (count, fine), 0)
+        hot = jnp.where(row == hot_ref[...], 1.0, 0.0).astype(BF16)
         wide = lax.broadcasted_iota(jnp.int32, (fine, 2 * TILE), 1) < TILE
         for v in range(LOADS):
             value = terms_ref[pl.ds(v, fine, stride=LOADS), :]
@@ -552,7 +556,6 @@
     )
     half_copy.start()
     half_copy.wait()
-    own = ROWS + HALF * h
     for t in range(HALF // 2):
         for j, other in zip((t, t + HALF // 2), unpack(half_in[t])):
             value = part_rows(mine, j) + other
@@ -585,15 +588,22 @@
     rows_loop(HALF, lambda j: apply_transposed(r_two[j], prol_two[j]), restrict_two)
     gathered(hot_two, terms_two, coarse_part, COARSE, HALF)
 
-    width = share * LOADS
-
-    def rows_of(member):
-        return pl.ds(pl.multiple_of(member * width, LOADS), width)
+    fold = 2 - share % 2
+    unit = share // fold
+
+    for c in range(size * unit):
+        member, r = c // unit, c % unit
+        first = (member * share + r) * LOADS
+        value = coarse_part[first : first + LOADS, :]
+        if fold == 2:
+            second = first + unit * LOADS
+            value = jnp.where(low, value, coarse_part[second : second + LOADS, :])
+        packed_c[member, r * LOADS : (r + 1) * LOADS] = value
 
     def copy_a(k):
         target = (e + k) % size
         return pltpu.make_async_remote_copy(
-            src_ref=coarse_part.at[rows_of(target)],
+            src_ref=packed_c.at[target],
             dst_ref=gather_a.at[k],
             send_sem=sem_a.at[0, k],
             recv_sem=sem_a.at[1, k],
@@ -603,7 +613,7 @@
 
     for k in range(1, size):
         copy_a(k).start()
-    total = coarse_part[rows_of(e), :]
+    total = packed_c[e]
     for k in range(1, size):
         copy_a(k).wait()
         total = total + gather_a[k]
@@ -627,12 +637,12 @@
     total = gather_b[0]
     for k in range(1, groups):
         total = total + gather_b[k]
-    full_c[rows_of(e), :] = total
+    full_c[e] = total
 
     def copy_c(k, member):
         return pltpu.make_async_remote_copy(
-            src_ref=full_c.at[rows_of(e)],
-            dst_ref=full_c.at[rows_of(member)],
+            src_ref=full_c.at[e],
+            dst_ref=full_c.at[member],
             send_sem=sem_c.at[0, k],
             recv_sem=sem_c.at[1, k],
             device_id=(g, (e + k) % size),
@@ -645,11 +655,15 @@
         copy_c(k, e).wait_send()
         copy_c(k, (e + size - k) % size).wait_recv()
 
-    for c in range(COARSE):
-        value = full_c[c * LOADS : (c + 1) * LOADS, :]
-        r_three[c] = value
-        d_three[0, c] = value / CENTER
-        coarse_ref[c] = value / CENTER
+    for c in range(size * unit):
+        member, r = c // unit, c % unit
+        value = full_c[member, r * LOADS : (r + 1) * LOADS]
+        values = unpack(value) if fold == 2 else (value,)
+        for k, value in enumerate(values):
+            row = member * share + r + k * unit
+            r_three[row] = value
+            d_three[0, row] = value / CENTER
+            coarse_ref[row] = value / CENTER
 
     for s, (old, new) in enumerate(COARSE_STEPS):
         now, later = s % 2, 1 - s % 2
@@ -659,8 +673,8 @@
                 r_three[c]
                 - apply_one(d_three[now, c], diag_three[c])
                 - apply_two(
-                    d_three[now, cols_three[c, 0]],
-                    d_three[now, cols_three[c, 1]],
+                    d_three[now, cols_three[0, c]],
+                    d_three[now, cols_three[1, c]],
                     offd_three[c],
                 )
             )
@@ -788,12 +802,11 @@
     offd_three,
 ):
     matrix, moves = (jnp.asarray(a, BF16) for a in spread())
-    hot_one = (agg_one[None, :] == jnp.arange(ROWS, dtype=jnp.int32)[:, None]).astype(BF16)
-    hot_two = (agg_two[None, :] == jnp.arange(COARSE, dtype=jnp.int32)[:, None]).astype(BF16)
     smem = pl.BlockSpec(memory_space=pltpu.SMEM)
     vmem = pl.BlockSpec(memory_space=pltpu.VMEM)
     row = (LOADS, 2 * TILE)
     share = COARSE // size
+    unit = share // (2 - share % 2) * LOADS
     dma = pltpu.SemaphoreType.DMA
     hbm = pl.BlockSpec(memory_space=pl.ANY)
     raw = [
@@ -815,7 +828,8 @@
             jax.ShapeDtypeStruct((COARSE, LOADS * TILE), F32),
         ),
         in_specs=[vmem] * 4
-        + [smem, hbm, hbm, hbm, smem, vmem] * 2
+        + [smem, hbm, hbm, hbm, smem, vmem]
+        + [smem, vmem, hbm, hbm, hbm, smem, vmem]
         + [smem, hbm, hbm],
         out_specs=(vmem, vmem),
         scratch_shapes=[pltpu.VMEM(a.shape, F32) for a in raw]
@@ -827,9 +841,9 @@
             pltpu.VMEM((6, 2, GHOST // 2, *row), F32),
             pltpu.VMEM((ROWS, *row), F32),
             pltpu.VMEM((ROWS, *row), F32),
-            pltpu.VMEM((6, 3 * ROWS, *row), F32),
-            pltpu.VMEM((6, HALF // 2, *row), F32),
-            pltpu.VMEM((6, 5, HALF // 2, *row), F32),
+            pltpu.VMEM((6, ROWS + 2 * HALF, *row), F32),
+            pltpu.VMEM((6, 3, HALF // 2, *row), F32),
+            pltpu.VMEM((6, 3, HALF // 2, *row), F32),
             pltpu.VMEM((HALF, *row), F32),
             pltpu.VMEM((HALF, *row), F32),
             pltpu.VMEM((HALF, *row), F32),
@@ -841,20 +855,23 @@
             pltpu.VMEM((ROWS, *row), F32),
             pltpu.VMEM((HALF * LOADS, 2 * TILE), F32),
             pltpu.VMEM((COARSE * LOADS, 2 * TILE), F32),
-            pltpu.VMEM((size, share * LOADS, 2 * TILE), F32),
-            pltpu.VMEM((groups, share * LOADS, 2 * TILE), F32),
-            pltpu.VMEM((COARSE * LOADS, 2 * TILE), F32),
+            pltpu.VMEM((size, unit, 2 * TILE), F32),
+            pltpu.VMEM((groups, unit, 2 * TILE), F32),
+            pltpu.VMEM((size, unit, 2 * TILE), F32),
+            pltpu.VMEM((size, unit, 2 * TILE), F32),
             pltpu.VMEM((2, COARSE, *row), F32),
             pltpu.VMEM((COARSE, *row), F32),
             pltpu.VMEM((COARSE, *row), F32),
             pltpu.VMEM((2, 2, GHOST), jnp.int32),
             pltpu.SMEM((2, 2, GHOST), jnp.int32),
+            pltpu.VMEM((2, 2, HALF), jnp.int32),
+            pltpu.SMEM((2, 2, HALF), jnp.int32),
             dma((8,)),
-            dma((3, 2)),
+            dma((3, 2, 2)),
             dma((6, 2)),
             dma((6, 2)),
-            dma((6, 5)),
-            dma((6, 5)),
+            dma((6, 3)),
+            dma((6, 3)),
             dma((2,)),
             dma((2,)),
             dma((2, size)),
@@ -869,15 +886,16 @@
         moves,
         right_side,
         ghost_rows,
-        cols_one,
+        cols_one.T,
         *raw[:3],
         agg_one,
-        hot_one,
-        cols_two,
+        agg_one[None],
+        cols_two.T,
+        cols_two.T,
         *raw[3:6],
         agg_two,
-        hot_two,
-        cols_three,
+        agg_two[None],
+        cols_three.T,
         *raw[6:],
     )
 

time: 161 us -> 148 us (0.919)
  Pallas kernels: 150 us -> 143 us
  local copies, waits for them, and re-layouts: 7.21 us -> 3.09 us
  other arithmetic: 2.53 us -> 0 us
    pallas_call x1, Pallas kernels: 150 us -> 143 us  [body(): pl.pallas_call(functools.partial(kernel, groups, size), out_shape=(jax.Sh...]
    unnamed x5 -> x2, local copies, waits for them, and re-layouts: 7.21 us -> 3.09 us
    convert_element_type x2 -> x0, other arithmetic: 2.53 us -> none  [the longest x1 1.27 us: body(): (agg_one[None, :] == jnp.arange(ROWS, dtype=jnp.int32)[:, None]).astype(B...]
where the time goes in v3:
time: 148 us; the launch traced here: 147 us
  Pallas kernels  143 us (97%)
  local copies, waits for them, and re-layouts  3.09 us (2%)
    pallas_call x1, Pallas kernels, body(): pl.pallas_call(functools.partial(kernel, groups, size), out_shape=(jax.Sh...  143 us
    unnamed x2, local copies, waits for them, and re-layouts  3.09 us

profile of v3, /device:TPU:29, one launch (start us, length us, event | category | flops | bytes accessed | tf_op | source)
XLA Modules:
  0.0 146.9 jit_solution(16047676148684635891)
XLA Ops:
  0.6 143.2 %shard_map.176 = (f32[96,512]{1,0:T(8,128)}, f32[32,512]{1,0:T(8,128)}) custom-call(bf16[256,256]{1,0:T(8,128)(2,1)} %constant.4.clone.matrix, bf16[3,128,128]{2,1,0:T(8,128)(2,1)} %constant.5.clone.moves, f32[96,512]{1,0:T(8,128)} %rhs_in.1, s32[2,24]{1,0:T(2,128)} %ghost_rows.1, s32[2,96]{1,0:T(2,128)} %bitcast.57, f32[3072,128]{1,0:T(8,128)} %bitcast.46, ...), custom_call_target="tpu_custom_call" | custom-call | tf_op jit(solution)/shard_map/pallas_call | solution.py:824
  143.8 1.6 %copy.24 = f32[96,512]{1,0:T(8,128)} copy(f32[96,512]{1,0:T(8,128)} %get-tuple-element.4) | data formatting | bytes 393216
  145.4 1.5 %copy.25 = f32[32,512]{1,0:T(8,128)} copy(f32[32,512]{1,0:T(8,128)} %get-tuple-element.5) | data formatting | bytes 131072
